TPU v7x, 32 devices: a whole 2x2x4 slice. The times are simulated.
32 devices in a mesh: grp: 8 (over y, x, core), ep: 4 (over z).
Axes of the slice: x: 2, y: 2, z: 4, core: 2. Of those that a mesh axis runs over, the one named last changes fastest.
Arguments:
- queries: bfloat16 [128, 2304], P('grp'), may hold values from -36 to 36, as said below
- residual: bfloat16 [128, 2304], P(('grp', 'ep')), may hold values from -20 to 20
- gain: bfloat16 [2304], replicated, may hold values from 0.5 to 1.5
- key_pages: bfloat16 [256, 128, 2304], P(('grp', 'ep')), may hold values from -6 to 6
- value_pages: bfloat16 [256, 128, 2304], P(('grp', 'ep')), may hold values from -6 to 6
- page_table: int32 [128, 16], P('grp'), may hold values from -1 to 31, as said below
- lengths: int32 [128], P('grp'), may hold values from 1 to 2048, as said below
- split_flag: int32 [128], P('grp'), may hold values from 0 to 1, as said below
- routes: int32 [128, 2], P(('grp', 'ep')), may hold values from 0 to 3, all different within a row; in each aligned block of 4 rows (0 to 3, 4 to 7, ...) at most 2 rows name the same one
- gates: bfloat16 [128, 2], P(('grp', 'ep')), may hold values from 0.19921875 to 1
- w_gate: bfloat16 [4, 2304, 5760], P('ep', None, 'grp'), may hold values from -0.125 to 0.125
- w_up: bfloat16 [4, 2304, 5760], P('ep', None, 'grp'), may hold values from -0.125 to 0.125
- w_down: bfloat16 [4, 5760, 2304], P('ep', 'grp'), may hold values from -0.078125 to 0.078125
Outputs:
- update: bfloat16 [128, 2304], P(('grp', 'ep'))
Inputs may be any that keep to these rules, and one draw needn't show every extreme that they name: `page_table`: entries j with j * 128 < lengths[r] are pages of the row's group; no page is named twice within a group; the other entries are -1. `lengths`: A split request's first half, in the even group of its pair, is always 16 * 128 tokens; other rows are no longer. `split_flag`: in every group exactly one row is 1, at the same slot in both groups of each pair 2i, 2i + 1. `routes`: within the rows of one device no expert is named more than 2 times. `queries`: the two rows of a split request hold the same query.
All inputs are finite; a program needn't handle non-finite values.
Results may differ from a plain program's by a relative error of at most 0.015.
Values may be sent and summed in bfloat16 or wider, within the bound.
A program may use at most 192 MiB of HBM per device.

v0:
```python
import jax
import jax.numpy as jnp
from jax import lax
from jax.sharding import PartitionSpec as P

HEAD_DIM = 64
PAGE = 128


NEG_FILL = -1e30
NORM_EPS = 1e-06


def joined_2(array, axis, combine):
    everything = jax.tree.map(lambda part: lax.all_gather(part, axis), array)
    leading = jax.tree.map(lambda part: part[0], everything)

    def turn(k, so_far):
        return combine(so_far, jax.tree.map(lambda part: part[k], everything))

    return lax.fori_loop(1, lax.axis_size(axis), turn, leading)


def from_partner(array, axis, bit):
    return lax.ppermute(array, axis, [(i, i ^ 1 << bit) for i in range(lax.axis_size(axis))])


def merge_parts(first_part, second_part):
    maxima_a, totals_a, weighted_a = first_part
    maxima_b, totals_b, weighted_b = second_part
    highest = jnp.maximum(maxima_a, maxima_b)
    factor_a = jnp.exp(maxima_a - highest)
    factor_b = jnp.exp(maxima_b - highest)
    head_count = maxima_a.shape[-1]
    shaped = weighted_a.shape
    wide = shaped[:-1] + (head_count, shaped[-1] // head_count)
    weighted = (
        weighted_a.reshape(wide) * factor_a[..., None]
        + weighted_b.reshape(wide) * factor_b[..., None]
    )
    return (highest, totals_a * factor_a + totals_b * factor_b, weighted.reshape(shaped))


def page_partials(group_q, page_rows, row_lengths, key_rows, value_rows, first_page):
    page_count = key_rows.shape[0]
    slot_count = group_q.shape[0]
    head_count = group_q.shape[1] // HEAD_DIM
    page_ids = first_page + jnp.arange(page_count, dtype=jnp.int32)
    table_steps = jnp.arange(page_rows.shape[1], dtype=jnp.int32)
    live_step = (table_steps * PAGE)[None, :] < row_lengths[:, None]
    matches = (page_rows[:, :, None] == page_ids[None, None, :]) & live_step[:, :, None]
    owned_page = jnp.any(matches, axis=1)
    where_at = jnp.sum(jnp.where(matches, table_steps[None, :, None], 0), axis=1)
    offsets = jnp.arange(PAGE, dtype=jnp.int32)
    token_pos = where_at[:, :, None] * PAGE + offsets[None, None, :]
    visible = (owned_page[:, :, None] & (token_pos < row_lengths[:, None, None])).reshape(
        slot_count, page_count * PAGE
    )
    query_heads = group_q.reshape(slot_count, head_count, HEAD_DIM)
    key_heads = key_rows.reshape(page_count * PAGE, head_count, HEAD_DIM)
    value_heads = value_rows.reshape(page_count * PAGE, head_count, HEAD_DIM)
    scores = jnp.einsum(
        "shd,khd->hsk", query_heads, key_heads, preferred_element_type=jnp.float32
    ) * HEAD_DIM ** (-0.5)
    scores = jnp.where(visible[None], scores, NEG_FILL)
    maxima = jnp.max(scores, axis=2)
    exp_terms = jnp.where(visible[None], jnp.exp(scores - maxima[..., None]), 0.0)
    totals = jnp.sum(exp_terms, axis=2)
    weights = exp_terms.astype(jnp.bfloat16)
    weighted = jnp.einsum("hsk,khd->shd", weights, value_heads, preferred_element_type=jnp.float32)
    return (maxima.T, totals.T, weighted.reshape(slot_count, head_count * HEAD_DIM))


def on_device(
    queries,
    residual,
    gain,
    key_pages,
    value_pages,
    page_table,
    lengths,
    split_flag,
    routes,
    gates,
    w_gate,
    w_up,
    w_down,
):
    req_dev = residual.shape[0]
    ep_size = lax.axis_size("ep")
    my_ep = lax.axis_index("ep")
    first_page = my_ep * key_pages.shape[0]
    maxima, totals, weighted = page_partials(
        queries, page_table, lengths, key_pages, value_pages, first_page
    )
    row_start = my_ep * req_dev
    merged = joined_2((maxima, totals, weighted), "ep", merge_parts)
    maxima = lax.dynamic_slice_in_dim(merged[0], row_start, req_dev, 0)
    totals = lax.dynamic_slice_in_dim(merged[1], row_start, req_dev, 0)
    weighted = lax.dynamic_slice_in_dim(merged[2], row_start, req_dev, 0)
    own_split = (lax.dynamic_slice_in_dim(split_flag, row_start, req_dev, 0) == 1)[:, None]
    partner = from_partner((maxima, totals, weighted), "grp", 0)
    joined = merge_parts((maxima, totals, weighted), partner)
    totals = jnp.where(own_split, joined[1], totals)
    weighted = jnp.where(own_split, joined[2], weighted)
    head_count = totals.shape[1]
    attn = (
        (weighted.reshape(req_dev, head_count, -1) / totals[..., None])
        .reshape(req_dev, -1)
        .astype(jnp.bfloat16)
    )
    stream = residual.astype(jnp.float32) + attn.astype(jnp.float32)
    normed = (
        stream
        * lax.rsqrt(jnp.mean(stream * stream, axis=-1, keepdims=True) + NORM_EPS)
        * gain.astype(jnp.float32)
    ).astype(jnp.bfloat16)
    capacity = max(2, (2 * req_dev + ep_size - 1) // ep_size)
    slot_count = ep_size * capacity
    chosen = routes.reshape(-1)
    one_hot = (chosen[:, None] == jnp.arange(ep_size, dtype=jnp.int32)[None, :]).astype(jnp.int32)
    ranking = jnp.sum((jnp.cumsum(one_hot, axis=0) - one_hot) * one_hot, axis=1)
    slot_of = chosen * capacity + ranking
    slot_ids = jnp.arange(slot_count, dtype=jnp.int32)
    placing = (slot_ids[:, None] == slot_of[None, :]).astype(jnp.bfloat16)
    doubled = jnp.repeat(normed, 2, axis=0)
    outgoing = (
        jnp.dot(placing, doubled, preferred_element_type=jnp.float32)
        .astype(jnp.bfloat16)
        .reshape(ep_size, capacity, -1)
    )
    arrived = lax.all_to_all(outgoing, "ep", split_axis=0, concat_axis=0, tiled=True).reshape(
        slot_count, -1
    )
    gate_matrix = w_gate[0]
    up_matrix = w_up[0]
    down_matrix = w_down[0]
    block_rows = lax.all_gather(arrived, "grp", axis=0, tiled=True)
    gate_part = jnp.dot(block_rows, gate_matrix, preferred_element_type=jnp.float32)
    up_part = jnp.dot(block_rows, up_matrix, preferred_element_type=jnp.float32)
    inner = (jax.nn.silu(gate_part) * up_part).astype(jnp.bfloat16)
    block_rows = inner
    summed = lax.psum_scatter(
        jnp.dot(block_rows, down_matrix, preferred_element_type=jnp.float32).astype(jnp.bfloat16),
        "grp",
        scatter_dimension=0,
        tiled=True,
    )
    results = summed.reshape(ep_size, capacity, -1)
    returned = lax.all_to_all(results, "ep", split_axis=0, concat_axis=0, tiled=True)
    picking = (slot_of[:, None] == slot_ids[None, :]).astype(jnp.float32) * gates.reshape(-1)[
        :, None
    ].astype(jnp.float32)
    blending = picking.reshape(req_dev, 2, slot_count).sum(axis=1).astype(jnp.bfloat16)
    mixture = jnp.dot(
        blending, returned.reshape(slot_count, -1), preferred_element_type=jnp.float32
    )
    return (attn.astype(jnp.float32) + mixture).astype(jnp.bfloat16)


def solution(mesh):
    in_specs = (
        P("grp", None),
        P(("grp", "ep"), None),
        P(),
        P(("grp", "ep"), None, None),
        P(("grp", "ep"), None, None),
        P("grp", None),
        P("grp"),
        P("grp"),
        P(("grp", "ep"), None),
        P(("grp", "ep"), None),
        P("ep", None, "grp"),
        P("ep", None, "grp"),
        P("ep", "grp", None),
    )
    out_specs = P(("grp", "ep"), None)
    return jax.shard_map(
        on_device, mesh=mesh, in_specs=in_specs, out_specs=out_specs, check_vma=False
    )
```

profile of v0, /device:TPU:0, one launch (start us, length us, event | category | flops | bytes accessed | tf_op | source)
XLA Modules:
  0.0 202.1 jit_solution(14815559593254437000)
XLA Ops:
  6.5 0.9 broadcast_compare_fusion
  7.4 1.2 select_reduce_fusion
  8.7 1.7 fusion.40
  11.6 7.1 %copy.60 = bf16[8,128,2304]{1,0,2:T(8,128)(2,1)} copy(bf16[8,128,2304]{2,1,0:T(8,128)(2,1)} %param.18) | data formatting | bytes 9437184 | tf_op args[3]
  18.7 8.2 %reshape.186 = bf16[1024,36,64]{0,2,1:T(8,128)(2,1)} reshape(bf16[8,128,2304]{1,0,2:T(8,128)(2,1)} %copy.60) | data formatting | bytes 9437184 | tf_op jit(solution)/shard_map/reshape | solution.py:60
  27.0 7.0 %copy.64 = bf16[8,128,2304]{1,0,2:T(8,128)(2,1)} copy(bf16[8,128,2304]{2,1,0:T(8,128)(2,1)} %param.19) | data formatting | bytes 9437184 | tf_op args[4]
  34.0 8.3 %reshape.187 = bf16[1024,36,64]{0,2,1:T(8,128)(2,1)} reshape(bf16[8,128,2304]{1,0,2:T(8,128)(2,1)} %copy.64) | data formatting | bytes 9437184 | tf_op jit(solution)/shard_map/reshape | solution.py:61
  42.6 3.3 %fusion.9 = (f32[36,16]{1,0:T(8,128)S(1)}, f32[36,16,1024]{2,1,0:T(8,128)S(1)}) fusion(pred[16,1024]{1,0:T(8,128)(4,1)S(1)} %fusion.39, bf16[1024,36,64]{0,2,1:T(8,128)(2,1)} %reshape.186, bf16[16,36,64]{2,1,0:T(8,128)(2,1)S(1)} %reshape.185), kind=kOutput, calls=%fused_computation.19 | convolution fusion | flops 77266368 | bytes 7170304 | tf_op jit(solution)/shard_map/shd,khd->hsk/dot_general | solution.py:62
  46.0 0.7 fusion.11
  46.7 1.4 fusion.19
  48.1 0.8 copy.65
  48.9 1.1 all_gather_reshape.3
  50.0 18.2 %all_gather.22 = f32[4,16,2304]{2,1,0:T(8,128)S(1)} all-gather(f32[1,16,2304]{2,1,0:T(8,128)S(1)} %all_gather_reshape.3), channel_id=1, replica_groups=mesh['grp'=8,'ep'=4] {'ep'}, dimensions={0}, use_global_device_ids=true | all-gather | bytes 737280 | tf_op jit(solution)/shard_map/all_gather | solution.py:15
  68.2 0.8 copy-done.1
  69.7 13.1 %all-gather.1 = f32[64,36]{1,0:T(8,128)S(1)} all-gather(f32[16,36]{1,0:T(8,128)S(1)} %copy.63), channel_id=3, replica_groups=mesh['grp'=8,'ep'=4] {'ep'}, dimensions={0}, use_global_device_ids=true | all-gather | bytes 11520 | tf_op jit(solution)/shard_map/all_gather | solution.py:15
  82.9 13.1 %all-gather = f32[64,36]{1,0:T(8,128)S(1)} all-gather(f32[16,36]{1,0:T(8,128)S(1)} %copy.62), channel_id=2, replica_groups=mesh['grp'=8,'ep'=4] {'ep'}, dimensions={0}, use_global_device_ids=true | all-gather | bytes 11520 | tf_op jit(solution)/shard_map/all_gather | solution.py:15
  96.0 19.1 %while.19 = (s32[]{:T(128)}, f32[16,36]{1,0:T(8,128)S(1)}, f32[16,36]{1,0:T(8,128)S(1)}, f32[16,2304]{1,0:T(8,128)}, f32[4,16,36]{2,1,0:T(8,128)S(1)}, /*index=5...) while((s32[]{:T(128)}, f32[16,36]{1,0:T(8,128)S(1)}, ...), condition=%wide.region_5.6_spmd, body=%wide.region_4.5_spmd.sunk | while | flops 114053 | bytes 1645207 | solution.py:21
  96.0 0.9 mul.275
  96.9 1.1 mul.276
  98.0 0.9 mul.277
  98.9 1.8 mul.278
  100.7 1.7 fusion.65
  102.4 0.9 mul.275
  103.3 1.1 mul.276
  104.4 0.9 mul.277
  105.3 1.8 mul.278
  107.0 1.7 fusion.65
  108.8 0.9 mul.275
  109.7 1.1 mul.276
  110.8 0.9 mul.277
  111.6 1.8 mul.278
  113.4 1.7 fusion.65
  115.7 1.5 constant_dynamic-slice_fusion.2
  117.3 0.8 copy.66
  118.8 0.7 dynamic-slice_compare_fusion
  120.9 1.1 multiply_reduce_fusion
  122.0 0.8 multiply_convert_fusion
  122.9 0.8 convolution_convert_fusion.1
  123.7 10.5 %all_to_all.10 = bf16[4,2,2304]{2,1,0:T(2,128)(2,1)S(1)} all-to-all(bf16[4,2,2304]{2,1,0:T(2,128)(2,1)S(1)} %reshape.189), channel_id=1, replica_groups=mesh['grp'=8,'ep'=4] {'ep'}, dimensions={0} | all-to-all | bytes 73728 | tf_op jit(solution)/shard_map/all_to_all | solution.py:132
  134.2 9.5 %all_gather.23 = bf16[64,2304]{1,0:T(8,128)(2,1)S(1)} all-gather(bf16[8,2304]{1,0:T(8,128)(2,1)S(1)} %reshape.190), channel_id=1, replica_groups=mesh['grp'=8,'ep'=4] {'grp'}, dimensions={0}, use_global_device_ids=true | all-gather | bytes 331776 | tf_op jit(solution)/shard_map/all_gather | solution.py:138
  143.6 0.7 copy-done.2
  144.3 3.0 %fusion.7 = f32[64,720]{1,0:T(8,128)S(1)} fusion(bf16[64,2304]{1,0:T(8,128)(2,1)S(1)} %all_gather.23, bf16[1,2304,720]{1,2,0:T(8,128)(2,1)} %param.25), kind=kOutput, calls=%fused_computation.15 | convolution fusion | flops 212336640 | bytes 3796992 | tf_op jit(solution)/shard_map/dot_general | solution.py:139
  147.4 4.9 %convolution_convert_fusion = bf16[64,2304]{1,0:T(8,128)(2,1)} fusion(bf16[1,720,2304]{2,1,0:T(8,128)(2,1)S(1)} %copy-done, bf16[64,2304]{1,0:T(8,128)(2,1)} %copy-done.2, bf16[1,2304,720]{1,2,0:T(8,128)(2,1)} %param.26, f32[64,720]{1,0:T(8,128)S(1)} %fusion.7), kind=kOutput, calls=%fused_computation.8 | convolution fusion | flops 425097216 | bytes 7409664 | tf_op jit(solution)/shard_map/dot_general | solution.py:144
  152.5 30.3 %reduce-scatter.2.cloned.1.call-done = bf16[8,2304]{1,0:T(8,128)(2,1)} async-done(((bf16[64,2304]{1,0:T(8,128)(2,1)}), bf16[8,2304]{1,0:T(8,128)(2,1)}) %reduce-scatter.2.cloned.1.call-update) | async-done | bytes 36880 | tf_op jit(solution)/shard_map/reduce_scatter | solution.py:143
  182.9 1.4 reshape.191
  184.3 4.6 %all-to-all-start.1 = ((bf16[4,2,2304]{2,1,0:T(2,128)(2,1)}), bf16[4,2,2304]{2,1,0:T(2,128)(2,1)S(1)}, u32[]{:S(2)}, u32[]{:S(2)}) async-start(bf16[4,2,2304]{2,1,0:T(2,128)(2,1)} %reshape.191), calls=%async_computation.2 | async-start | bytes 73728 | tf_op jit(solution)/shard_map/all_to_all | solution.py:150
  188.9 5.6 %all-to-all-done.1 = bf16[4,2,2304]{2,1,0:T(2,128)(2,1)S(1)} async-done(((bf16[4,2,2304]{2,1,0:T(2,128)(2,1)}), bf16[4,2,2304]{2,1,0:T(2,128)(2,1)S(1)}, u32[]{:S(2)}, u32[]{:S(2)}) %all-to-all-start.1) | async-done | bytes 36896 | tf_op jit(solution)/shard_map/all_to_all | solution.py:150
  194.5 0.7 fusion.3
  (71 shorter events, 5.6 us)
Async XLA Ops:
  6.5 140.9 %copy-start = (bf16[1,720,2304]{2,1,0:T(8,128)(2,1)S(1)}, bf16[1,720,2304]{2,1,0:T(8,128)(2,1)}, u32[]{:S(2)}) copy-start(bf16[1,720,2304]{2,1,0:T(8,128)(2,1)} %param.27) | copy-start | bytes 9953284
  6.5 176.3 %reduce-scatter.2.cloned.1.call-start = ((), (), s32[]{:S(2)}) async-start(), calls=%async_computation.3 | async-start | bytes 331776 | tf_op jit(solution)/shard_map/reduce_scatter | solution.py:143
  18.7 8.2 %copy-start.3 = (bf16[16,2304]{1,0:T(8,128)(2,1)S(1)}, bf16[16,2304]{1,0:T(8,128)(2,1)}, u32[]{:S(2)}) copy-start(bf16[16,2304]{1,0:T(8,128)(2,1)} %param.15) | copy-start | bytes 221188
  34.0 8.3 %copy-start.4 = (s32[16,8]{1,0:T(8,128)S(1)}, s32[16,8]{1,0:T(8,128)}, u32[]{:S(2)}) copy-start(s32[16,8]{1,0:T(8,128)} %broadcast_multiply_fusion) | copy-start | bytes 1540
  34.0 8.4 %copy-start.6 = (pred[16,8]{1,0:T(8,128)(4,1)S(1)}, pred[16,8]{1,0:T(8,128)(4,1)}, u32[]{:S(2)}) copy-start(pred[16,8]{1,0:T(8,128)(4,1)} %fusion.40) | copy-start | bytes 388
  34.0 8.5 %copy-start.5 = (s32[1024]{0:T(1024)S(1)}, s32[1024]{0:T(1024)}, u32[]{:S(2)}) copy-start(s32[1024]{0:T(1024)} %iota_bitcast_fusion) | copy-start | bytes 12292
  34.0 8.5 %copy-start.7 = (s32[16]{0:T(128)S(1)}, s32[16]{0:T(128)}, u32[]{:S(2)}) copy-start(s32[16]{0:T(128)} %param.21) | copy-start | bytes 196
  42.5 4.1 %slice-start = ((s8[4718592]{0:T(1024)(128)(4,1)}), s8[4194304]{0:T(1024)(128)(4,1)S(1)}, s32[]{:S(2)}) async-start(s8[4718592]{0:T(1024)(128)(4,1)} %bitcast.65), calls=%async_computation.4 | async-start | bytes 8388608
  42.6 4.1 %slice-start.1 = ((s8[4718592]{0:T(1024)(128)(4,1)}), s8[524288]{0:T(1024)(128)(4,1)S(1)}, s32[]{:S(2)}) async-start(s8[4718592]{0:T(1024)(128)(4,1)} %bitcast.65), calls=%async_computation.5 | async-start | bytes 1048576
  68.2 0.8 copy-start.1
  115.1 5.1 %collective-permute-start = (f32[4,36]{1,0:T(4,128)S(1)}, f32[4,36]{1,0:T(4,128)S(1)}, u32[]{:S(2)}, u32[]{:S(2)}) collective-permute-start(f32[4,36]{1,0:T(4,128)S(1)} %constant_dynamic-slice_fusion.1), channel_id=1, source_target_pairs={{0,4},{4,0},{8,12},{12,8},{16,20},{20,16},{24,28},{28,24},{1,5},{5... | collective-permute-start | bytes 1736 | tf_op jit(solution)/shard_map/ppermute | solution.py:25
  115.2 5.1 %collective-permute-start.2 = (f32[4,36]{1,0:T(4,128)S(1)}, f32[4,36]{1,0:T(4,128)S(1)}, u32[]{:S(2)}, u32[]{:S(2)}) collective-permute-start(f32[4,36]{1,0:T(4,128)S(1)} %constant_dynamic-slice_fusion), channel_id=1, source_target_pairs={{0,4},{4,0},{8,12},{12,8},{16,20},{20,16},{24,28},{28,24},{1,5},{5... | collective-permute-start | bytes 1736 | tf_op jit(solution)/shard_map/ppermute | solution.py:25
  117.2 3.7 %collective-permute-start.1 = (f32[4,2304]{1,0:T(4,128)}, f32[4,2304]{1,0:T(4,128)}, u32[]{:S(2)}, u32[]{:S(2)}) collective-permute-start(f32[4,2304]{1,0:T(4,128)} %constant_dynamic-slice_fusion.2), channel_id=1, source_target_pairs={{0,4},{4,0},{8,12},{12,8},{16,20},{20,16},{24,28},{28,24},{1,5},{5... | collective-permute-start | bytes 110600 | tf_op jit(solution)/shard_map/ppermute | solution.py:25
  143.6 0.7 copy-start.2
  147.4 5.1 %copy-start.8 = (bf16[4,2]{0,1:T(2,128)(2,1)S(1)}, bf16[4,2]{0,1:T(2,128)(2,1)}, u32[]{:S(2)}) copy-start(bf16[4,2]{0,1:T(2,128)(2,1)} %param.24) | copy-start | bytes 52
  184.3 10.3 %all-to-all-start.1 = ((bf16[4,2,2304]{2,1,0:T(2,128)(2,1)}), bf16[4,2,2304]{2,1,0:T(2,128)(2,1)S(1)}, u32[]{:S(2)}, u32[]{:S(2)}) async-start(bf16[4,2,2304]{2,1,0:T(2,128)(2,1)} %reshape.191), calls=%async_computation.2 | async-start | bytes 73728 | tf_op jit(solution)/shard_map/all_to_all | solution.py:150
Sparse Core Ops, SparseCore 0:
  152.4 30.3 reduce-scatter.1
where the time goes:
time: 204 us; the launch traced here: 202 us
  blocking collectives  64.3 us (32%)
  local copies, waits for them, and re-layouts  54.2 us (27%)
  waiting for transfers between devices  35.9 us (18%)
  other arithmetic  14.7 us (7%)
  matrix products  14.2 us (7%)
  between operations  13.6 us (7%)
  starting transfers between devices  5.17 us (3%)
    all_gather x3, blocking collectives, joined_2(): everything = jax.tree.map(lambda part: lax.all_gather(part, axis), array)  44.4 us
    reduce_scatter x1, waiting for transfers between devices, on_device(): lax.psum_scatter(jnp.dot(block_rows, down_matrix, preferred_element_type=...  30.3 us
    unnamed x25, local copies, waits for them, and re-layouts  16.4 us
    all_to_all x1, blocking collectives, on_device(): lax.all_to_all(outgoing, 'ep', split_axis=0, concat_axis=0, tiled=True)  10.5 us
    all_gather x1, blocking collectives, on_device(): block_rows = lax.all_gather(arrived, 'grp', axis=0, tiled=True)  9.45 us
    reshape x1, local copies, waits for them, and re-layouts, page_partials(): value_heads = value_rows.reshape(page_count * PAGE, head_count, HEAD_DIM)  8.27 us
    reshape x1, local copies, waits for them, and re-layouts, page_partials(): key_heads = key_rows.reshape(page_count * PAGE, head_count, HEAD_DIM)  8.2 us
    mul x8, local copies, waits for them, and re-layouts, merge_parts(): weighted_a.reshape(wide) * factor_a[..., None]  8.07 us
  transfers between devices with their start and end apart: 5, of which 2 were waited for; matrix products, arithmetic and copies ran while one was open for 3% of the time, Pallas kernels for 0%

commit v1 on v0

v1 whole, which is shorter than its diff:
```python
import functools

import jax
import jax.numpy as jnp
from jax import lax
from jax.experimental import pallas as pl
from jax.experimental.pallas import tpu as pltpu
from jax.sharding import PartitionSpec as P

HEAD_DIM = 64
PAGE = 128
LANES = 128
NEG_FILL = -1e30
NEG_FLOOR = -1e29
NORM_EPS = 1e-06
TOP = 2
B_COLS = 384

F32 = jnp.float32
BF16 = jnp.bfloat16


def iota(shape, axis):
    return lax.broadcasted_iota(jnp.int32, shape, axis)


def dot(a, b, contract=((1,), (0,))):
    return lax.dot_general(a, b, (contract, ((), ())), preferred_element_type=F32)


def fused(
    sizes,
    q_ref, res_ref, gain_ref, pt_ref, routes_ref, gates_ref,
    len_ref, split_ref,
    key_hbm, value_hbm, wg_hbm, wu_hbm, wd_hbm,
    out_ref,
    kbuf, vbuf, wg, wu, wd,
    e_ref, hm_ref, qp_ref, lim_ref, st_ref, w_ref, own_ref, o_ref,
    pw_ref, rs_ref, rt_ref,
    r_all, st_all, a_all, b_send, b_recv, x_all, y_send, y_recv, z_send, z_recv,
    kv_sem, w_sem,
    r_ss, r_rs, st_ss, st_rs, a_ss, a_rs, b_ss, b_rs, x_ss, x_rs, y_ss, y_rs, z_ss, z_rs,
):
    n_grp, n_ep, cap = sizes
    req_dev, D = res_ref.shape
    R = q_ref.shape[0]
    J = pt_ref.shape[1]
    PD = key_hbm.shape[0]
    half = D // 2
    heads = D // HEAD_DIM
    HP = hm_ref.shape[0]
    slots = n_ep * cap
    NPP = own_ref.shape[0]
    n_pages = n_ep * PD

    g = lax.axis_index("grp")
    e = lax.axis_index("ep")
    mate = g + 1 - 2 * lax.rem(g, 2)

    ep_peers = [lax.rem(e + k, n_ep) for k in range(1, n_ep)]
    grp_peers = [lax.rem(g + k, n_grp) for k in range(1, n_grp)]

    barrier = pltpu.get_barrier_semaphore()
    for peer in ep_peers:
        pl.semaphore_signal(barrier, inc=1, device_id=(g, peer), device_id_type=pl.DeviceIdType.MESH)
    for peer in grp_peers:
        pl.semaphore_signal(barrier, inc=1, device_id=(peer, e), device_id_type=pl.DeviceIdType.MESH)
    for peer in ep_peers:
        pl.semaphore_signal(barrier, inc=1, device_id=(mate, peer), device_id_type=pl.DeviceIdType.MESH)

    def kv_copies(p):
        return (
            pltpu.make_async_copy(key_hbm.at[p], kbuf.at[p], kv_sem.at[0, p]),
            pltpu.make_async_copy(value_hbm.at[p], vbuf.at[p], kv_sem.at[1, p]),
        )

    for p in range(PD):
        for copy in kv_copies(p):
            copy.start()
    w_copies = [
        pltpu.make_async_copy(wg_hbm.at[0], wg, w_sem.at[0]),
        pltpu.make_async_copy(wu_hbm.at[0], wu, w_sem.at[1]),
        pltpu.make_async_copy(wd_hbm.at[0], wd, w_sem.at[2]),
    ]
    for copy in w_copies:
        copy.start()

    def remote(src, dst, ss, rs, device):
        return pltpu.make_async_remote_copy(
            src_ref=src, dst_ref=dst, send_sem=ss, recv_sem=rs,
            device_id=device, device_id_type=pl.DeviceIdType.MESH,
        )

    res = res_ref[...].astype(F32)
    r_all[e, 0:req_dev, 0:half] = res[:, :half]
    r_all[e, req_dev:2 * req_dev, 0:half] = res[:, half:]
    route_lane = iota((2 * req_dev, LANES), 1)
    routes = routes_ref[...]
    routes_f = routes.astype(F32)
    r_all[e, :, half:half + LANES] = jnp.zeros((2 * req_dev, LANES), F32)
    r_all[e, 0:req_dev, half:half + LANES] = jnp.where(
        route_lane[:req_dev] == 0, routes_f[:, 0:1],
        jnp.where(route_lane[:req_dev] == 1, routes_f[:, 1:2], 0.0),
    )
    pl.semaphore_wait(barrier, 2 * (n_ep - 1) + n_grp - 1)
    r_sends = [
        remote(r_all.at[e], r_all.at[e], r_ss.at[k], r_rs.at[e], (g, peer))
        for k, peer in enumerate(ep_peers)
    ]
    for copy in r_sends:
        copy.start()

    first_col = iota((LANES, D), 0) * HEAD_DIM
    col = iota((LANES, D), 1)
    in_head = (col >= first_col) & (col < first_col + HEAD_DIM)
    e_ref[...] = jnp.where(in_head, 1.0, 0.0).astype(BF16)
    hm_ref[...] = jnp.where(in_head[:HP], 1.0, 0.0)
    st_ref[...] = jnp.zeros_like(st_ref)
    pw_ref[...] = jnp.zeros_like(pw_ref)

    split_row = 0
    for r in range(R):
        split_row = split_row + jnp.where(split_ref[r] == 1, r, 0)

    page_id = iota((NPP, J), 0)
    j_start = iota((1, J), 1) * PAGE
    local_id = iota((PD, J), 0) + e * PD
    owner = jnp.full((NPP, J), -1.0, F32)
    own_local = jnp.full((PD, J), -1.0, F32)
    limit = jnp.zeros((PD, J), F32)
    length_col = jnp.zeros((R, 1), jnp.int32)
    split_col = jnp.zeros((R, 1), jnp.int32)
    row_col = iota((R, 1), 0)
    for r in range(R):
        length = len_ref[r]
        entries = jnp.where(j_start < length, pt_ref[r:r + 1, :], -1)
        owner = jnp.where(page_id == entries, float(r), owner)
        hit = local_id == entries
        own_local = jnp.where(hit, float(r), own_local)
        limit = jnp.where(hit, jnp.minimum(length - j_start, PAGE).astype(F32), limit)
        length_col = jnp.where(row_col == r, length, length_col)
        split_col = jnp.where(row_col == r, split_ref[r], split_col)
    owner = jnp.max(owner, axis=1, keepdims=True)
    page_col = iota((NPP, LANES), 0)
    mate_pages = (page_col >= n_pages) & (page_col < n_pages + n_ep)
    own_ref[...] = jnp.where(
        mate_pages, split_row.astype(F32), jnp.broadcast_to(owner, (NPP, LANES))
    )
    own_local = jnp.max(own_local, axis=1, keepdims=True)
    limit = jnp.sum(limit, axis=1, keepdims=True)
    lim_ref[...] = jnp.broadcast_to(limit, (PD, LANES))
    split_local = jnp.broadcast_to(own_local, (PD, LANES)) == split_row.astype(F32)

    page_lane = iota((R, NPP), 1)
    o_rows = jnp.where(
        (page_lane >= n_pages) & (page_lane < n_pages + n_ep) & (split_col == 1), 1.0, 0.0
    )
    for j in range(J):
        entry = jnp.where(length_col > j * PAGE, pt_ref[:, j:j + 1], -1)
        o_rows = jnp.where(page_lane == entry, 1.0, o_rows)
    o_ref[...] = o_rows.astype(BF16)

    queries = q_ref[...].astype(F32)
    page_q = jnp.zeros((PD, D), F32)
    for r in range(R):
        page_q = jnp.where(own_local == float(r), queries[r:r + 1, :], page_q)
    qp_ref[...] = page_q

    token = iota((1, LANES), 1).astype(F32)
    stat_lane = iota((HP, LANES), 1)

    def page_step(p):
        for copy in kv_copies(p):
            copy.wait()
        q_page = qp_ref[pl.ds(p, 1), :]
        q_heads = (jnp.broadcast_to(q_page, (HP, D)) * hm_ref[...]).astype(BF16)
        scores = dot(q_heads, kbuf[p], ((1,), (1,))) * HEAD_DIM ** (-0.5)
        visible = token < lim_ref[pl.ds(p, 1), :]
        scores = jnp.where(visible, scores, NEG_FILL)
        top = jnp.maximum(jnp.max(scores, axis=1, keepdims=True), NEG_FLOOR)
        terms = jnp.exp(scores - top)
        total = jnp.sum(terms, axis=1, keepdims=True)
        st_ref[0:HP, :] = jnp.where(stat_lane == p, top, st_ref[0:HP, :])
        st_ref[64:64 + HP, :] = jnp.where(stat_lane == p, total, st_ref[64:64 + HP, :])
        wide = dot(terms.astype(BF16), vbuf[p])
        w_ref[pl.ds(p, 1), :] = jnp.sum(wide * hm_ref[...], axis=0, keepdims=True)

    def pages(i, carry):
        page_step(2 * i)
        page_step(2 * i + 1)
        return carry

    lax.fori_loop(0, PD // 2, pages, 0)

    head_lane = iota((1, LANES), 1) < heads

    weighted = w_ref[...]
    a_all[e] = jnp.concatenate([weighted[:, :half], weighted[:, half:]], axis=0).astype(BF16)
    stats = jnp.transpose(st_ref[...])[0:PD, :]
    st_all[e] = stats
    exchange = []
    for k, peer in enumerate(ep_peers):
        exchange.append(remote(a_all.at[e], a_all.at[e], a_ss.at[k], a_rs.at[e], (g, peer)))
        exchange.append(remote(st_all.at[e], st_all.at[e], st_ss.at[k], st_rs.at[e], (g, peer)))
    for copy in exchange:
        copy.start()

    totals = pltpu.roll(stats, 64, 1)
    split_top = jnp.max(jnp.where(split_local, stats, NEG_FILL), axis=0, keepdims=True)
    factor = jnp.where(split_local & head_lane, jnp.exp(stats - split_top), 0.0)
    split_total = jnp.sum(factor * totals, axis=0, keepdims=True)
    part = jnp.sum(dot(factor.astype(BF16), e_ref[...]) * weighted, axis=0, keepdims=True)
    b_send[...] = jnp.zeros_like(b_send)
    b_rows = D // B_COLS
    for i in range(b_rows):
        b_send[i:i + 1, :] = part[:, i * B_COLS:(i + 1) * B_COLS]
    b_send[b_rows:b_rows + 1, 0:LANES] = split_top
    b_send[b_rows:b_rows + 1, LANES:2 * LANES] = split_total
    b_targets = [e] + ep_peers
    b_sends = [
        remote(b_send, b_recv.at[e], b_ss.at[k], b_rs.at[e], (mate, peer))
        for k, peer in enumerate(b_targets)
    ]
    for copy in b_sends:
        copy.start()

    for src in ep_peers:
        remote(r_all.at[src], r_all.at[src], r_ss.at[0], r_rs.at[src], (g, src)).wait_recv()
    for s in range(n_ep):
        rows = slice(s * req_dev, (s + 1) * req_dev)
        rs_ref[rows, 0:half] = r_all[s, 0:req_dev, 0:half]
        rs_ref[rows, half:D] = r_all[s, req_dev:2 * req_dev, 0:half]
        rt_ref[rows, :] = r_all[s, 0:req_dev, half:half + LANES]

    expert = e.astype(F32)
    chosen = rt_ref[...]
    has_col = jnp.where((chosen[:, 0:1] == expert) | (chosen[:, 1:2] == expert), 1.0, 0.0)
    r_sub = iota((R, R), 0)
    r_lane = iota((R, R), 1)
    has_row = jnp.sum(jnp.where(r_sub == r_lane, has_col, 0.0), axis=0, keepdims=True)
    earlier = (r_sub < r_lane) & (r_sub // req_dev == r_lane // req_dev)
    rank_row = jnp.sum(jnp.where(earlier, has_col, 0.0), axis=0, keepdims=True)
    slot_sub = iota((slots, R), 0)
    slot_row = iota((slots, R), 1)
    pick = jnp.where(
        (slot_sub // cap == slot_row // req_dev)
        & (has_row > 0.5)
        & (rank_row == (slot_sub % cap).astype(F32)),
        1.0, 0.0,
    ).astype(BF16)

    slot_lane = iota((req_dev, LANES), 1)
    first_hit = slot_lane // cap == routes[:, 0:1]
    second_hit = slot_lane // cap == routes[:, 1:2]
    gates = gates_ref[...].astype(F32)
    hits = jnp.where(first_hit | second_hit, 1.0, 0.0)
    row_sub = iota((req_dev, LANES), 0)
    rank = jnp.zeros((req_dev, LANES), F32)
    for i in range(req_dev - 1):
        rank = rank + jnp.where(row_sub > i, hits[i:i + 1, :], 0.0)
    blend = jnp.where(first_hit, gates[:, 0:1], 0.0) + jnp.where(second_hit, gates[:, 1:2], 0.0)
    blend = jnp.where(rank == (slot_lane % cap).astype(F32), blend, 0.0)

    for src in ep_peers:
        remote(st_all.at[src], st_all.at[src], st_ss.at[0], st_rs.at[src], (g, src)).wait_recv()
    for src in b_targets:
        remote(b_send, b_recv.at[src], b_ss.at[0], b_rs.at[src], (mate, src)).wait_recv()
    extra = NPP - n_pages
    extra_sub = iota((extra, LANES), 0)
    extra_top = jnp.full((extra, LANES), NEG_FILL, F32)
    extra_total = jnp.zeros((extra, LANES), F32)
    for s in range(n_ep):
        extra_top = jnp.where(extra_sub == s, b_recv[s, b_rows:b_rows + 1, 0:LANES], extra_top)
        extra_total = jnp.where(
            extra_sub == s, b_recv[s, b_rows:b_rows + 1, LANES:2 * LANES], extra_total
        )
        for i in range(b_rows):
            pw_ref[s:s + 1, i * B_COLS:(i + 1) * B_COLS] = b_recv[s, i:i + 1, :]
    all_stats = st_all[...].reshape(n_pages, LANES)
    all_top = jnp.concatenate([all_stats, extra_top], axis=0)
    all_total = jnp.concatenate([pltpu.roll(all_stats, 64, 1), extra_total], axis=0)
    owners = own_ref[...]
    row_top = jnp.zeros((NPP, LANES), F32)
    for r in range(R):
        mine = owners == float(r)
        highest = jnp.max(jnp.where(mine, all_top, NEG_FILL), axis=0, keepdims=True)
        row_top = jnp.where(mine, highest, row_top)
    owned = (owners >= 0.0) & head_lane
    scale = jnp.where(owned, jnp.exp(jnp.where(owned, all_top - row_top, 0.0)), 0.0)
    scaled_total = scale * all_total
    row_total = jnp.ones((NPP, LANES), F32)
    for r in range(R):
        mine = owners == float(r)
        summed = jnp.sum(jnp.where(mine, scaled_total, 0.0), axis=0, keepdims=True)
        row_total = jnp.where(mine, summed, row_total)
    share = jnp.where(owned, scale / jnp.where(owned, row_total, 1.0), 0.0).astype(BF16)

    for src in ep_peers:
        remote(a_all.at[src], a_all.at[src], a_ss.at[0], a_rs.at[src], (g, src)).wait_recv()
    parts = a_all[...].astype(F32)
    attn = []
    for h in range(2):
        columns = slice(h * half, (h + 1) * half)
        own_pages = parts[:, h * PD:(h + 1) * PD, :].reshape(n_pages, half)
        values = jnp.concatenate([own_pages, pw_ref[:, columns]], axis=0)
        terms = (dot(share, e_ref[:, columns]) * values).astype(BF16)
        attn.append(dot(o_ref[...], terms).astype(BF16))
    stream = [rs_ref[:, h * half:(h + 1) * half] + attn[h].astype(F32) for h in range(2)]
    square = sum(jnp.sum(s * s, axis=1, keepdims=True) for s in stream) * (1.0 / D)
    inverse = lax.rsqrt(square + NORM_EPS)
    normed = [
        (stream[h] * inverse * gain_ref[:, h * half:(h + 1) * half].astype(F32)).astype(BF16)
        for h in range(2)
    ]
    x_all[g] = jnp.concatenate([dot(pick, n) for n in normed], axis=0).astype(BF16)

    x_sends = [
        remote(x_all.at[g], x_all.at[g], x_ss.at[k], x_rs.at[g], (peer, e))
        for k, peer in enumerate(grp_peers)
    ]
    for copy in x_sends:
        copy.start()
    own_pick = jnp.where(iota((req_dev, R), 1) == iota((req_dev, R), 0) + e * req_dev, 1.0, 0.0)
    own_attn = [dot(own_pick.astype(BF16), a) for a in attn]
    for copy in w_copies:
        copy.wait()
    for src in grp_peers:
        remote(x_all.at[src], x_all.at[src], x_ss.at[0], x_rs.at[src], (src, e)).wait_recv()

    rows_in = x_all[...].astype(F32)
    x_lo = rows_in[:, :slots, :].reshape(n_grp * slots, half).astype(BF16)
    x_hi = rows_in[:, slots:, :].reshape(n_grp * slots, half).astype(BF16)
    gate_part = dot(x_lo, wg[0:half, :]) + dot(x_hi, wg[half:D, :])
    up_part = dot(x_lo, wu[0:half, :]) + dot(x_hi, wu[half:D, :])
    inner = (gate_part / (1.0 + jnp.exp(-gate_part)) * up_part).astype(BF16)
    for h in range(2):
        y_half = dot(inner, wd[:, h * half:(h + 1) * half])
        y_send[:, h * slots:(h + 1) * slots, :] = y_half.reshape(n_grp, slots, half).astype(BF16)

    y_sends = [
        remote(y_send.at[peer], y_recv.at[g], y_ss.at[k], y_rs.at[g], (peer, e))
        for k, peer in enumerate(grp_peers)
    ]
    for copy in y_sends:
        copy.start()
    summed = y_send[g].astype(F32)
    for src in grp_peers:
        remote(y_send.at[src], y_recv.at[src], y_ss.at[0], y_rs.at[src], (src, e)).wait_recv()
        summed = summed + y_recv[src].astype(F32)
    summed = summed.astype(BF16).astype(F32)

    for s in range(n_ep):
        z_send[s, 0:cap, :] = summed[s * cap:(s + 1) * cap, :]
        z_send[s, cap:2 * cap, :] = summed[slots + s * cap:slots + (s + 1) * cap, :]
    z_sends = [
        remote(z_send.at[peer], z_recv.at[e], z_ss.at[k], z_rs.at[e], (g, peer))
        for k, peer in enumerate(ep_peers)
    ]
    for copy in z_sends:
        copy.start()
    z_recv[e] = z_send[e]
    for src in ep_peers:
        remote(z_send.at[src], z_recv.at[src], z_ss.at[0], z_rs.at[src], (g, src)).wait_recv()
    for h in range(2):
        update = own_attn[h]
        for s in range(n_ep):
            for c in range(cap):
                slot = s * cap + c
                update = update + blend[:, slot:slot + 1] * z_recv[s, h * cap + c:h * cap + c + 1, :]
        out_ref[:, h * half:(h + 1) * half] = update.astype(BF16)

    for copy in r_sends + exchange + b_sends + x_sends + y_sends + z_sends:
        copy.wait_send()


def on_device(
    n_grp, n_ep,
    queries, residual, gain, key_pages, value_pages, page_table, lengths, split_flag,
    routes, gates, w_gate, w_up, w_down,
):
    req_dev, D = residual.shape
    R = queries.shape[0]
    PD = key_pages.shape[0]
    F = w_gate.shape[2]
    half = D // 2
    heads = D // HEAD_DIM
    HP = -(-heads // 8) * 8
    cap = max(2, (TOP * req_dev + n_ep - 1) // n_ep)
    slots = n_ep * cap
    n_pages = n_ep * PD
    NPP = -(-(n_pages + n_ep) // 16) * 16
    vmem = pl.BlockSpec(memory_space=pltpu.VMEM)
    smem = pl.BlockSpec(memory_space=pltpu.SMEM)
    hbm = pl.BlockSpec(memory_space=pl.ANY)
    dma = pltpu.SemaphoreType.DMA
    scratch = [
        pltpu.VMEM((PD, PAGE, D), BF16),
        pltpu.VMEM((PD, PAGE, D), BF16),
        pltpu.VMEM((D, F), BF16),
        pltpu.VMEM((D, F), BF16),
        pltpu.VMEM((F, D), BF16),
        pltpu.VMEM((LANES, D), BF16),
        pltpu.VMEM((HP, D), F32),
        pltpu.VMEM((PD, D), F32),
        pltpu.VMEM((PD, LANES), F32),
        pltpu.VMEM((LANES, LANES), F32),
        pltpu.VMEM((PD, D), F32),
        pltpu.VMEM((NPP, LANES), F32),
        pltpu.VMEM((R, NPP), BF16),
        pltpu.VMEM((NPP - n_pages, D), F32),
        pltpu.VMEM((R, D), F32),
        pltpu.VMEM((R, LANES), F32),
        pltpu.VMEM((n_ep, 2 * req_dev, half + LANES), F32),
        pltpu.VMEM((n_ep, PD, LANES), F32),
        pltpu.VMEM((n_ep, 2 * PD, half), BF16),
        pltpu.VMEM((8, B_COLS), F32),
        pltpu.VMEM((n_ep, 8, B_COLS), F32),
        pltpu.VMEM((n_grp, 2 * slots, half), BF16),
        pltpu.VMEM((n_grp, 2 * slots, half), BF16),
        pltpu.VMEM((n_grp, 2 * slots, half), BF16),
        pltpu.VMEM((n_ep, 2 * cap, half), F32),
        pltpu.VMEM((n_ep, 2 * cap, half), F32),
        dma((2, PD)),
        dma((3,)),
    ]
    for senders, receivers in (
        (n_ep, n_ep), (n_ep, n_ep), (n_ep, n_ep), (n_ep, n_ep), (n_grp, n_grp), (n_grp, n_grp), (n_ep, n_ep)
    ):
        scratch += [dma((senders,)), dma((receivers,))]
    return pl.pallas_call(
        functools.partial(fused, (n_grp, n_ep, cap)),
        out_shape=jax.ShapeDtypeStruct((req_dev, D), BF16),
        in_specs=[vmem] * 6 + [smem] * 2 + [hbm] * 5,
        out_specs=vmem,
        scratch_shapes=scratch,
        compiler_params=pltpu.CompilerParams(
            collective_id=0, has_side_effects=True, vmem_limit_bytes=56 * 1024 * 1024
        ),
    )(
        queries, residual, gain.reshape(1, D), page_table, routes, gates,
        lengths, split_flag,
        key_pages, value_pages, w_gate, w_up, w_down,
    )


def solution(mesh):
    in_specs = (
        P("grp", None),
        P(("grp", "ep"), None),
        P(),
        P(("grp", "ep"), None, None),
        P(("grp", "ep"), None, None),
        P("grp", None),
        P("grp"),
        P("grp"),
        P(("grp", "ep"), None),
        P(("grp", "ep"), None),
        P("ep", None, "grp"),
        P("ep", None, "grp"),
        P("ep", "grp", None),
    )
    return jax.shard_map(
        functools.partial(on_device, mesh.shape["grp"], mesh.shape["ep"]),
        mesh=mesh, in_specs=in_specs, out_specs=P(("grp", "ep"), None), check_vma=False,
    )
```

time: 204 us -> 53.5 us (0.26)
  blocking collectives: 64.3 us -> 0 us
  local copies, waits for them, and re-layouts: 54.2 us -> 14.8 us
  Pallas kernels: 0 us -> 38.3 us
  waiting for transfers between devices: 35.9 us -> 0 us
  other arithmetic: 14.7 us -> 0 us
  matrix products: 14.2 us -> 0 us
  between operations: 13.6 us -> 0.01 us
  starting transfers between devices: 5.17 us -> 0 us
    all_gather x4 -> x0, blocking collectives: 53.9 us -> none  [the longest x3 44.4 us: joined_2(): everything = jax.tree.map(lambda part: lax.all_gather(part, axis), array)]
    pallas_call x0 -> x1, Pallas kernels: none -> 38.3 us  [on_device(): pl.pallas_call(functools.partial(fused, (n_grp, n_ep, cap)), out_shape=ja...]
    reduce_scatter x1 -> x0, waiting for transfers between devices: 30.3 us -> none  [on_device(): lax.psum_scatter(jnp.dot(block_rows, down_matrix, preferred_element_type=...]
    reshape x8 -> x1, local copies, waits for them, and re-layouts: 18.1 us -> 1.3 us  [on_device(): gain.reshape(1, D)]
    dot_general x6 -> x0, matrix products: 14.2 us -> none  [the longest x1 4.89 us: on_device(): jnp.dot(block_rows, down_matrix, preferred_element_type=jnp.float32)]
    mul x16 -> x0, local copies, waits for them, and re-layouts: 14.2 us -> none  [the longest x8 8.07 us: merge_parts(): weighted_a.reshape(wide) * factor_a[..., None]]
    all_to_all x1 -> x0, blocking collectives: 10.5 us -> none  [on_device(): lax.all_to_all(outgoing, 'ep', split_axis=0, concat_axis=0, tiled=True)]
    add x9 -> x0, other arithmetic: 5.8 us -> none  [the longest x3 5.23 us: merge_parts(): weighted_a.reshape(wide) * factor_a[..., None]]
  transfers between devices with their start and end apart: 5 -> 0, of which waited for: 2 -> 0; matrix products, arithmetic and copies ran while one was open for 3% -> 0% of each run, Pallas kernels for 0% -> 0%
where the time goes in v1:
time: 53.5 us; the launch traced here: 53.1 us
  Pallas kernels  38.3 us (72%)
  local copies, waits for them, and re-layouts  14.8 us (28%)
    pallas_call x1, Pallas kernels, on_device(): pl.pallas_call(functools.partial(fused, (n_grp, n_ep, cap)), out_shape=ja...  38.3 us
    unnamed x7, local copies, waits for them, and re-layouts  13.5 us
    reshape x1, local copies, waits for them, and re-layouts, on_device(): gain.reshape(1, D)  1.3 us

profile of v1, /device:TPU:0, one launch (start us, length us, event | category | flops | bytes accessed | tf_op | source)
XLA Modules:
  0.0 53.1 jit_solution(15839487809999450398)
XLA Ops:
  0.0 0.0 copy-start
  0.0 1.5 %copy.15.gates_ref = bf16[4,2]{1,0:T(4,128)(2,1)} copy(bf16[4,2]{0,1:T(2,128)(2,1)} %param.22) | data formatting | bytes 32 | tf_op args[9]
  1.5 1.3 %copy.14.routes_ref = s32[4,2]{1,0:T(4,128)} copy(s32[4,2]{0,1:T(2,128)} %param.21) | data formatting | bytes 64 | tf_op args[8]
  2.8 1.3 %reshape.3.gain_ref = bf16[1,2304]{1,0:T(2,128)(2,1)} reshape(bf16[2304]{0:T(1024)(128)(2,1)} %param.15) | data formatting | bytes 9216 | tf_op jit(solution)/shard_map/reshape | solution.py:440
  4.1 5.7 %copy.16.wg_hbm = bf16[1,2304,720]{2,1,0:T(8,128)(2,1)} copy(bf16[1,2304,720]{1,2,0:T(8,128)(2,1)} %param.23) | data formatting | bytes 6635520 | tf_op args[10]
  9.8 0.0 copy-done
  9.8 3.6 %copy.17.wu_hbm = bf16[1,2304,720]{2,1,0:T(8,128)(2,1)} copy(bf16[1,2304,720]{1,2,0:T(8,128)(2,1)S(1)} %copy-done) | data formatting | bytes 6635520 | tf_op args[11]
  13.4 38.3 %shard_map.127 = bf16[4,2304]{1,0:T(4,128)(2,1)} custom-call(bf16[16,2304]{1,0:T(8,128)(2,1)} %q_ref.1, bf16[4,2304]{1,0:T(4,128)(2,1)} %res_ref.1, bf16[1,2304]{1,0:T(2,128)(2,1)} %reshape.3.gain_ref, s32[16,16]{1,0:T(8,128)} %pt_ref.1, s32[4,2]{1,0:T(4,128)} %copy.14.routes_ref, bf16[4,2]{1,0:T(4,128)(2,1)} %copy.15.gates_ref, s32[16]{0:T(128)} %len_ref.1, ...), custom_call_target="tpu_custom_call" | custom-call | tf_op jit(solution)/shard_map/pallas_call | solution.py:430
  51.8 1.3 %copy.19 = bf16[4,2304]{1,0:T(4,128)(2,1)} copy(bf16[4,2304]{1,0:T(4,128)(2,1)} %shard_map.127) | data formatting | bytes 36864
Async XLA Ops:
  0.0 9.8 %copy-start = (bf16[1,2304,720]{1,2,0:T(8,128)(2,1)S(1)}, bf16[1,2304,720]{1,2,0:T(8,128)(2,1)}, u32[]{:S(2)}) copy-start(bf16[1,2304,720]{1,2,0:T(8,128)(2,1)} %param.24) | copy-start | bytes 9953284

commit v2 on v1

--- a/solution.py
+++ b/solution.py
@@ -15,6 +15,7 @@
 NORM_EPS = 1e-06
 TOP = 2
 B_COLS = 384
+CHUNKS = 3
 
 F32 = jnp.float32
 BF16 = jnp.bfloat16
@@ -95,12 +96,19 @@
     r_all[e, 0:req_dev, 0:half] = res[:, :half]
     r_all[e, req_dev:2 * req_dev, 0:half] = res[:, half:]
     route_lane = iota((2 * req_dev, LANES), 1)
-    routes = routes_ref[...]
-    routes_f = routes.astype(F32)
+    eye = iota((req_dev, req_dev), 0) == iota((req_dev, req_dev), 1)
+
+    def column(row):
+        return jnp.sum(jnp.where(eye, row, 0.0), axis=1, keepdims=True)
+
+    routes_t = routes_ref[...].astype(F32)
+    gates_t = gates_ref[...].astype(F32)
+    routes = [column(routes_t[k:k + 1, :]) for k in range(TOP)]
+    gates = [column(gates_t[k:k + 1, :]) for k in range(TOP)]
     r_all[e, :, half:half + LANES] = jnp.zeros((2 * req_dev, LANES), F32)
     r_all[e, 0:req_dev, half:half + LANES] = jnp.where(
-        route_lane[:req_dev] == 0, routes_f[:, 0:1],
-        jnp.where(route_lane[:req_dev] == 1, routes_f[:, 1:2], 0.0),
+        route_lane[:req_dev] == 0, routes[0],
+        jnp.where(route_lane[:req_dev] == 1, routes[1], 0.0),
     )
     pl.semaphore_wait(barrier, 2 * (n_ep - 1) + n_grp - 1)
     r_sends = [
@@ -250,15 +258,15 @@
     ).astype(BF16)
 
     slot_lane = iota((req_dev, LANES), 1)
-    first_hit = slot_lane // cap == routes[:, 0:1]
-    second_hit = slot_lane // cap == routes[:, 1:2]
-    gates = gates_ref[...].astype(F32)
+    slot_expert = (slot_lane // cap).astype(F32)
+    first_hit = slot_expert == routes[0]
+    second_hit = slot_expert == routes[1]
     hits = jnp.where(first_hit | second_hit, 1.0, 0.0)
     row_sub = iota((req_dev, LANES), 0)
     rank = jnp.zeros((req_dev, LANES), F32)
     for i in range(req_dev - 1):
         rank = rank + jnp.where(row_sub > i, hits[i:i + 1, :], 0.0)
-    blend = jnp.where(first_hit, gates[:, 0:1], 0.0) + jnp.where(second_hit, gates[:, 1:2], 0.0)
+    blend = jnp.where(first_hit, gates[0], 0.0) + jnp.where(second_hit, gates[1], 0.0)
     blend = jnp.where(rank == (slot_lane % cap).astype(F32), blend, 0.0)
 
     for src in ep_peers:
@@ -307,9 +315,10 @@
         attn.append(dot(o_ref[...], terms).astype(BF16))
     stream = [rs_ref[:, h * half:(h + 1) * half] + attn[h].astype(F32) for h in range(2)]
     square = sum(jnp.sum(s * s, axis=1, keepdims=True) for s in stream) * (1.0 / D)
+    gain = gain_ref[...].astype(F32).reshape(1, D)
     inverse = lax.rsqrt(square + NORM_EPS)
     normed = [
-        (stream[h] * inverse * gain_ref[:, h * half:(h + 1) * half].astype(F32)).astype(BF16)
+        (stream[h] * inverse * gain[:, h * half:(h + 1) * half]).astype(BF16)
         for h in range(2)
     ]
     x_all[g] = jnp.concatenate([dot(pick, n) for n in normed], axis=0).astype(BF16)
@@ -330,44 +339,63 @@
     rows_in = x_all[...].astype(F32)
     x_lo = rows_in[:, :slots, :].reshape(n_grp * slots, half).astype(BF16)
     x_hi = rows_in[:, slots:, :].reshape(n_grp * slots, half).astype(BF16)
-    gate_part = dot(x_lo, wg[0:half, :]) + dot(x_hi, wg[half:D, :])
-    up_part = dot(x_lo, wu[0:half, :]) + dot(x_hi, wu[half:D, :])
+    last = ((1,), (1,))
+    gate_part = dot(x_lo, wg[:, 0:half], last) + dot(x_hi, wg[:, half:D], last)
+    up_part = dot(x_lo, wu[:, 0:half], last) + dot(x_hi, wu[:, half:D], last)
     inner = (gate_part / (1.0 + jnp.exp(-gate_part)) * up_part).astype(BF16)
-    for h in range(2):
-        y_half = dot(inner, wd[:, h * half:(h + 1) * half])
-        y_send[:, h * slots:(h + 1) * slots, :] = y_half.reshape(n_grp, slots, half).astype(BF16)
-
-    y_sends = [
-        remote(y_send.at[peer], y_recv.at[g], y_ss.at[k], y_rs.at[g], (peer, e))
-        for k, peer in enumerate(grp_peers)
-    ]
-    for copy in y_sends:
-        copy.start()
-    summed = y_send[g].astype(F32)
-    for src in grp_peers:
-        remote(y_send.at[src], y_recv.at[src], y_ss.at[0], y_rs.at[src], (src, e)).wait_recv()
-        summed = summed + y_recv[src].astype(F32)
-    summed = summed.astype(BF16).astype(F32)
-
-    for s in range(n_ep):
-        z_send[s, 0:cap, :] = summed[s * cap:(s + 1) * cap, :]
-        z_send[s, cap:2 * cap, :] = summed[slots + s * cap:slots + (s + 1) * cap, :]
-    z_sends = [
-        remote(z_send.at[peer], z_recv.at[e], z_ss.at[k], z_rs.at[e], (g, peer))
-        for k, peer in enumerate(ep_peers)
-    ]
-    for copy in z_sends:
-        copy.start()
-    z_recv[e] = z_send[e]
-    for src in ep_peers:
-        remote(z_send.at[src], z_recv.at[src], z_ss.at[0], z_rs.at[src], (g, src)).wait_recv()
-    for h in range(2):
-        update = own_attn[h]
+
+    width = D // CHUNKS
+    piece = width // 2
+    y_sends = []
+    for c in range(CHUNKS):
+        y_part = dot(inner, wd[:, c * width:(c + 1) * width])
+        for h in range(2):
+            y_send[c, :, h * slots:(h + 1) * slots, :] = (
+                y_part[:, h * piece:(h + 1) * piece].reshape(n_grp, slots, piece).astype(BF16)
+            )
+        sends = [
+            remote(y_send.at[c, peer], y_recv.at[c, g], y_ss.at[c, k], y_rs.at[c, g], (peer, e))
+            for k, peer in enumerate(grp_peers)
+        ]
+        for copy in sends:
+            copy.start()
+        y_sends += sends
+
+    z_sends = []
+    for c in range(CHUNKS):
+        summed = y_send[c, g].astype(F32)
+        for src in grp_peers:
+            remote(
+                y_send.at[c, src], y_recv.at[c, src], y_ss.at[c, 0], y_rs.at[c, src], (src, e)
+            ).wait_recv()
+            summed = summed + y_recv[c, src].astype(F32)
+        summed = summed.astype(BF16).astype(F32)
         for s in range(n_ep):
-            for c in range(cap):
-                slot = s * cap + c
-                update = update + blend[:, slot:slot + 1] * z_recv[s, h * cap + c:h * cap + c + 1, :]
-        out_ref[:, h * half:(h + 1) * half] = update.astype(BF16)
+            z_send[c, s, 0:cap, :] = summed[s * cap:(s + 1) * cap, :]
+            z_send[c, s, cap:2 * cap, :] = summed[slots + s * cap:slots + (s + 1) * cap, :]
+        sends = [
+            remote(z_send.at[c, peer], z_recv.at[c, e], z_ss.at[c, k], z_rs.at[c, e], (g, peer))
+            for k, peer in enumerate(ep_peers)
+        ]
+        for copy in sends:
+            copy.start()
+        z_recv[c, e] = z_send[c, e]
+        z_sends += sends
+    own_both = jnp.concatenate(own_attn, axis=1)
+    for c in range(CHUNKS):
+        for src in ep_peers:
+            remote(
+                z_send.at[c, src], z_recv.at[c, src], z_ss.at[c, 0], z_rs.at[c, src], (g, src)
+            ).wait_recv()
+        for h in range(2):
+            start = c * width + h * piece
+            update = own_both[:, start:start + piece]
+            for s in range(n_ep):
+                for i in range(cap):
+                    slot = s * cap + i
+                    row = h * cap + i
+                    update = update + blend[:, slot:slot + 1] * z_recv[c, s, row:row + 1, :]
+            out_ref[:, start:start + piece] = update.astype(BF16)
 
     for copy in r_sends + exchange + b_sends + x_sends + y_sends + z_sends:
         copy.wait_send()
@@ -396,8 +424,8 @@
     scratch = [
         pltpu.VMEM((PD, PAGE, D), BF16),
         pltpu.VMEM((PD, PAGE, D), BF16),
-        pltpu.VMEM((D, F), BF16),
-        pltpu.VMEM((D, F), BF16),
+        pltpu.VMEM((F, D), BF16),
+        pltpu.VMEM((F, D), BF16),
         pltpu.VMEM((F, D), BF16),
         pltpu.VMEM((LANES, D), BF16),
         pltpu.VMEM((HP, D), F32),
@@ -416,17 +444,17 @@
         pltpu.VMEM((8, B_COLS), F32),
         pltpu.VMEM((n_ep, 8, B_COLS), F32),
         pltpu.VMEM((n_grp, 2 * slots, half), BF16),
-        pltpu.VMEM((n_grp, 2 * slots, half), BF16),
-        pltpu.VMEM((n_grp, 2 * slots, half), BF16),
-        pltpu.VMEM((n_ep, 2 * cap, half), F32),
-        pltpu.VMEM((n_ep, 2 * cap, half), F32),
+        pltpu.VMEM((CHUNKS, n_grp, 2 * slots, half // CHUNKS), BF16),
+        pltpu.VMEM((CHUNKS, n_grp, 2 * slots, half // CHUNKS), BF16),
+        pltpu.VMEM((CHUNKS, n_ep, 2 * cap, half // CHUNKS), F32),
+        pltpu.VMEM((CHUNKS, n_ep, 2 * cap, half // CHUNKS), F32),
         dma((2, PD)),
         dma((3,)),
     ]
-    for senders, receivers in (
-        (n_ep, n_ep), (n_ep, n_ep), (n_ep, n_ep), (n_ep, n_ep), (n_grp, n_grp), (n_grp, n_grp), (n_ep, n_ep)
+    for shape in (
+        (n_ep,), (n_ep,), (n_ep,), (n_ep,), (n_grp,), (CHUNKS, n_grp), (CHUNKS, n_ep)
     ):
-        scratch += [dma((senders,)), dma((receivers,))]
+        scratch += [dma(shape), dma(shape)]
     return pl.pallas_call(
         functools.partial(fused, (n_grp, n_ep, cap)),
         out_shape=jax.ShapeDtypeStruct((req_dev, D), BF16),
@@ -437,9 +465,9 @@
             collective_id=0, has_side_effects=True, vmem_limit_bytes=56 * 1024 * 1024
         ),
     )(
-        queries, residual, gain.reshape(1, D), page_table, routes, gates,
+        queries, residual, gain, page_table, routes.T, gates.T,
         lengths, split_flag,
-        key_pages, value_pages, w_gate, w_up, w_down,
+        key_pages, value_pages, jnp.swapaxes(w_gate, 1, 2), jnp.swapaxes(w_up, 1, 2), w_down,
     )
 
 

time: 53.5 us -> 40.6 us (0.76)
  local copies, waits for them, and re-layouts: 14.8 us -> 1.34 us
  Pallas kernels: 38.3 us -> 39.1 us
    unnamed x7 -> x1, local copies, waits for them, and re-layouts: 13.5 us -> 1.34 us
    reshape x1 -> x0, local copies, waits for them, and re-layouts: 1.3 us -> none  [on_device(): gain.reshape(1, D)]
    pallas_call x1, Pallas kernels: 38.3 us -> 39.1 us  [on_device(): pl.pallas_call(functools.partial(fused, (n_grp, n_ep, cap)), out_shape=ja...]
where the time goes in v2:
time: 40.6 us; the launch traced here: 40.4 us
  Pallas kernels  39.1 us (96%)
  local copies, waits for them, and re-layouts  1.34 us (3%)
    pallas_call x1, Pallas kernels, on_device(): pl.pallas_call(functools.partial(fused, (n_grp, n_ep, cap)), out_shape=ja...  39.1 us
    unnamed x1, local copies, waits for them, and re-layouts  1.34 us

profile of v2, /device:TPU:0, one launch (start us, length us, event | category | flops | bytes accessed | tf_op | source)
XLA Modules:
  0.0 40.4 jit_solution(6809963015213280284)
XLA Ops:
  0.0 39.1 %shard_map.127 = bf16[4,2304]{1,0:T(4,128)(2,1)} custom-call(bf16[16,2304]{1,0:T(8,128)(2,1)} %q_ref.1, bf16[4,2304]{1,0:T(4,128)(2,1)} %res_ref.1, bf16[2304]{0:T(1024)(128)(2,1)} %gain_ref.1, s32[16,16]{1,0:T(8,128)} %pt_ref.1, s32[2,4]{1,0:T(2,128)} %bitcast.6, bf16[2,4]{1,0:T(2,128)(2,1)} %bitcast.7, s32[16]{0:T(128)} %len_ref.1, s32[16]{0:T(128)} %split_ref.1, ...), custom_call_target="tpu_custom_call" | custom-call | tf_op jit(solution)/shard_map/pallas_call | solution.py:458
  39.1 1.3 %copy.15 = bf16[4,2304]{1,0:T(4,128)(2,1)} copy(bf16[4,2304]{1,0:T(4,128)(2,1)} %shard_map.127) | data formatting | bytes 36864

commit v3 on v2

--- a/solution.py
+++ b/solution.py
@@ -16,6 +16,8 @@
 TOP = 2
 B_COLS = 384
 CHUNKS = 3
+QUARTERS = ((0, 640), (640, 1280), (1280, 1792), (1792, 2304))
+PART_COLS = 640
 
 F32 = jnp.float32
 BF16 = jnp.bfloat16
@@ -37,10 +39,10 @@
     out_ref,
     kbuf, vbuf, wg, wu, wd,
     e_ref, hm_ref, qp_ref, lim_ref, st_ref, w_ref, own_ref, o_ref,
-    pw_ref, rs_ref, rt_ref,
-    r_all, st_all, a_all, b_send, b_recv, x_all, y_send, y_recv, z_send, z_recv,
+    wv_ref, af_ref, rs_ref, rt_ref,
+    r_all, st_all, a_all, b_send, b_recv, x_all, y_send, y_pair, y_sum, y_recv, z_send, z_recv,
     kv_sem, w_sem,
-    r_ss, r_rs, st_ss, st_rs, a_ss, a_rs, b_ss, b_rs, x_ss, x_rs, y_ss, y_rs, z_ss, z_rs,
+    r_ss, r_rs, st_ss, st_rs, a_ss, a_rs, b_ss, b_rs, x_ss, x_rs, p_ss, p_rs, y_ss, y_rs, z_ss, z_rs,
 ):
     n_grp, n_ep, cap = sizes
     req_dev, D = res_ref.shape
@@ -59,14 +61,21 @@
     mate = g + 1 - 2 * lax.rem(g, 2)
 
     ep_peers = [lax.rem(e + k, n_ep) for k in range(1, n_ep)]
-    grp_peers = [lax.rem(g + k, n_grp) for k in range(1, n_grp)]
+    pairs = n_grp // 2
+    side = lax.rem(g, 2)
+    pair = lax.div(g, 2)
+    pair_peers = [lax.rem(pair + k, pairs) for k in range(1, pairs)]
+    mine_first, mate_first = side * pairs, (1 - side) * pairs
+    my_place = mine_first + pair
 
     barrier = pltpu.get_barrier_semaphore()
     for peer in ep_peers:
         pl.semaphore_signal(barrier, inc=1, device_id=(g, peer), device_id_type=pl.DeviceIdType.MESH)
-    for peer in grp_peers:
-        pl.semaphore_signal(barrier, inc=1, device_id=(peer, e), device_id_type=pl.DeviceIdType.MESH)
-    for peer in ep_peers:
+    for peer in pair_peers:
+        pl.semaphore_signal(
+            barrier, inc=1, device_id=(2 * peer + side, e), device_id_type=pl.DeviceIdType.MESH
+        )
+    for peer in [e] + ep_peers:
         pl.semaphore_signal(barrier, inc=1, device_id=(mate, peer), device_id_type=pl.DeviceIdType.MESH)
 
     def kv_copies(p):
@@ -83,8 +92,6 @@
         pltpu.make_async_copy(wu_hbm.at[0], wu, w_sem.at[1]),
         pltpu.make_async_copy(wd_hbm.at[0], wd, w_sem.at[2]),
     ]
-    for copy in w_copies:
-        copy.start()
 
     def remote(src, dst, ss, rs, device):
         return pltpu.make_async_remote_copy(
@@ -110,7 +117,7 @@
         route_lane[:req_dev] == 0, routes[0],
         jnp.where(route_lane[:req_dev] == 1, routes[1], 0.0),
     )
-    pl.semaphore_wait(barrier, 2 * (n_ep - 1) + n_grp - 1)
+    pl.semaphore_wait(barrier, 2 * n_ep - 1 + pairs - 1)
     r_sends = [
         remote(r_all.at[e], r_all.at[e], r_ss.at[k], r_rs.at[e], (g, peer))
         for k, peer in enumerate(ep_peers)
@@ -124,7 +131,7 @@
     e_ref[...] = jnp.where(in_head, 1.0, 0.0).astype(BF16)
     hm_ref[...] = jnp.where(in_head[:HP], 1.0, 0.0)
     st_ref[...] = jnp.zeros_like(st_ref)
-    pw_ref[...] = jnp.zeros_like(pw_ref)
+    wv_ref[n_pages:, :] = jnp.zeros((NPP - n_pages, D), F32)
 
     split_row = 0
     for r in range(R):
@@ -198,26 +205,44 @@
         page_step(2 * i + 1)
         return carry
 
-    lax.fori_loop(0, PD // 2, pages, 0)
+    part_pages = PD // 2
+    af_ref[...] = jnp.zeros_like(af_ref)
+    exchange = []
+
+    def send_part(c):
+        for i, (low, high) in enumerate(QUARTERS):
+            af_ref[i * part_pages:(i + 1) * part_pages, 0:high - low] = (
+                w_ref[c * part_pages:(c + 1) * part_pages, low:high]
+            )
+        a_all[c, e] = af_ref[...].astype(BF16)
+        for k, peer in enumerate(ep_peers):
+            copy = remote(
+                a_all.at[c, e], a_all.at[c, e], a_ss.at[c, k], a_rs.at[c, e], (g, peer)
+            )
+            copy.start()
+            exchange.append(copy)
+
+    lax.fori_loop(0, PD // 4, pages, 0)
+    send_part(0)
+    lax.fori_loop(PD // 4, PD // 2, pages, 0)
+    for copy in w_copies:
+        copy.start()
+    send_part(1)
 
     head_lane = iota((1, LANES), 1) < heads
 
-    weighted = w_ref[...]
-    a_all[e] = jnp.concatenate([weighted[:, :half], weighted[:, half:]], axis=0).astype(BF16)
     stats = jnp.transpose(st_ref[...])[0:PD, :]
     st_all[e] = stats
-    exchange = []
     for k, peer in enumerate(ep_peers):
-        exchange.append(remote(a_all.at[e], a_all.at[e], a_ss.at[k], a_rs.at[e], (g, peer)))
-        exchange.append(remote(st_all.at[e], st_all.at[e], st_ss.at[k], st_rs.at[e], (g, peer)))
-    for copy in exchange:
+        copy = remote(st_all.at[e], st_all.at[e], st_ss.at[k], st_rs.at[e], (g, peer))
         copy.start()
+        exchange.append(copy)
 
     totals = pltpu.roll(stats, 64, 1)
     split_top = jnp.max(jnp.where(split_local, stats, NEG_FILL), axis=0, keepdims=True)
     factor = jnp.where(split_local & head_lane, jnp.exp(stats - split_top), 0.0)
     split_total = jnp.sum(factor * totals, axis=0, keepdims=True)
-    part = jnp.sum(dot(factor.astype(BF16), e_ref[...]) * weighted, axis=0, keepdims=True)
+    part = jnp.sum(dot(factor.astype(BF16), e_ref[...]) * w_ref[...], axis=0, keepdims=True)
     b_send[...] = jnp.zeros_like(b_send)
     b_rows = D // B_COLS
     for i in range(b_rows):
@@ -283,7 +308,8 @@
             extra_sub == s, b_recv[s, b_rows:b_rows + 1, LANES:2 * LANES], extra_total
         )
         for i in range(b_rows):
-            pw_ref[s:s + 1, i * B_COLS:(i + 1) * B_COLS] = b_recv[s, i:i + 1, :]
+            row = n_pages + s
+            wv_ref[row:row + 1, i * B_COLS:(i + 1) * B_COLS] = b_recv[s, i:i + 1, :]
     all_stats = st_all[...].reshape(n_pages, LANES)
     all_top = jnp.concatenate([all_stats, extra_top], axis=0)
     all_total = jnp.concatenate([pltpu.roll(all_stats, 64, 1), extra_total], axis=0)
@@ -303,15 +329,22 @@
         row_total = jnp.where(mine, summed, row_total)
     share = jnp.where(owned, scale / jnp.where(owned, row_total, 1.0), 0.0).astype(BF16)
 
-    for src in ep_peers:
-        remote(a_all.at[src], a_all.at[src], a_ss.at[0], a_rs.at[src], (g, src)).wait_recv()
-    parts = a_all[...].astype(F32)
+    for c in range(2):
+        for src in ep_peers:
+            remote(
+                a_all.at[c, src], a_all.at[c, src], a_ss.at[c, 0], a_rs.at[c, src], (g, src)
+            ).wait_recv()
+        for s in range(n_ep):
+            arrived = a_all[c, s].astype(F32)
+            first = s * PD + c * part_pages
+            for i, (low, high) in enumerate(QUARTERS):
+                wv_ref[first:first + part_pages, low:high] = (
+                    arrived[i * part_pages:(i + 1) * part_pages, 0:high - low]
+                )
     attn = []
     for h in range(2):
         columns = slice(h * half, (h + 1) * half)
-        own_pages = parts[:, h * PD:(h + 1) * PD, :].reshape(n_pages, half)
-        values = jnp.concatenate([own_pages, pw_ref[:, columns]], axis=0)
-        terms = (dot(share, e_ref[:, columns]) * values).astype(BF16)
+        terms = (dot(share, e_ref[:, columns]) * wv_ref[:, columns]).astype(BF16)
         attn.append(dot(o_ref[...], terms).astype(BF16))
     stream = [rs_ref[:, h * half:(h + 1) * half] + attn[h].astype(F32) for h in range(2)]
     square = sum(jnp.sum(s * s, axis=1, keepdims=True) for s in stream) * (1.0 / D)
@@ -321,20 +354,28 @@
         (stream[h] * inverse * gain[:, h * half:(h + 1) * half]).astype(BF16)
         for h in range(2)
     ]
-    x_all[g] = jnp.concatenate([dot(pick, n) for n in normed], axis=0).astype(BF16)
+    x_all[my_place] = jnp.concatenate([dot(pick, n) for n in normed], axis=0).astype(BF16)
+
+    def x_copy(place, k, device):
+        return remote(x_all.at[place], x_all.at[place], x_ss.at[k], x_rs.at[place], device)
 
     x_sends = [
-        remote(x_all.at[g], x_all.at[g], x_ss.at[k], x_rs.at[g], (peer, e))
-        for k, peer in enumerate(grp_peers)
+        x_copy(my_place, k, (2 * peer + side, e)) for k, peer in enumerate(pair_peers)
     ]
+    x_sends.append(x_copy(my_place, pairs - 1, (mate, e)))
     for copy in x_sends:
         copy.start()
     own_pick = jnp.where(iota((req_dev, R), 1) == iota((req_dev, R), 0) + e * req_dev, 1.0, 0.0)
     own_attn = [dot(own_pick.astype(BF16), a) for a in attn]
+    for k, peer in enumerate(pair_peers):
+        x_copy(mine_first + peer, 0, (mate, e)).wait_recv()
+        forward = x_copy(mine_first + peer, pairs + k, (mate, e))
+        forward.start()
+        x_sends.append(forward)
     for copy in w_copies:
         copy.wait()
-    for src in grp_peers:
-        remote(x_all.at[src], x_all.at[src], x_ss.at[0], x_rs.at[src], (src, e)).wait_recv()
+    for peer in [pair] + pair_peers:
+        x_copy(mate_first + peer, 0, (mate, e)).wait_recv()
 
     rows_in = x_all[...].astype(F32)
     x_lo = rows_in[:, :slots, :].reshape(n_grp * slots, half).astype(BF16)
@@ -347,26 +388,44 @@
     width = D // CHUNKS
     piece = width // 2
     y_sends = []
+
+    def pair_copy(c):
+        return remote(
+            y_send.at[c, pl.ds(mate_first, pairs)], y_pair.at[c], p_ss.at[c], p_rs.at[c], (mate, e)
+        )
+
+    def pair_sum(c):
+        pair_copy(c).wait_recv()
+        both = y_send[c, pl.ds(mine_first, pairs)].astype(F32) + y_pair[c].astype(F32)
+        y_sum[c] = both.astype(BF16)
+        for k, peer in enumerate(pair_peers):
+            copy = remote(
+                y_sum.at[c, peer], y_recv.at[c, pair], y_ss.at[c, k], y_rs.at[c, pair],
+                (2 * peer + side, e),
+            )
+            copy.start()
+            y_sends.append(copy)
+
     for c in range(CHUNKS):
         y_part = dot(inner, wd[:, c * width:(c + 1) * width])
         for h in range(2):
             y_send[c, :, h * slots:(h + 1) * slots, :] = (
                 y_part[:, h * piece:(h + 1) * piece].reshape(n_grp, slots, piece).astype(BF16)
             )
-        sends = [
-            remote(y_send.at[c, peer], y_recv.at[c, g], y_ss.at[c, k], y_rs.at[c, g], (peer, e))
-            for k, peer in enumerate(grp_peers)
-        ]
-        for copy in sends:
-            copy.start()
-        y_sends += sends
+        copy = pair_copy(c)
+        copy.start()
+        y_sends.append(copy)
+        if c:
+            pair_sum(c - 1)
+    pair_sum(CHUNKS - 1)
 
     z_sends = []
     for c in range(CHUNKS):
-        summed = y_send[c, g].astype(F32)
-        for src in grp_peers:
+        summed = y_sum[c, pair].astype(F32)
+        for src in pair_peers:
             remote(
-                y_send.at[c, src], y_recv.at[c, src], y_ss.at[c, 0], y_rs.at[c, src], (src, e)
+                y_sum.at[c, src], y_recv.at[c, src], y_ss.at[c, 0], y_rs.at[c, src],
+                (2 * src + side, e),
             ).wait_recv()
             summed = summed + y_recv[c, src].astype(F32)
         summed = summed.astype(BF16).astype(F32)
@@ -435,24 +494,28 @@
         pltpu.VMEM((PD, D), F32),
         pltpu.VMEM((NPP, LANES), F32),
         pltpu.VMEM((R, NPP), BF16),
-        pltpu.VMEM((NPP - n_pages, D), F32),
+        pltpu.VMEM((NPP, D), F32),
+        pltpu.VMEM((2 * PD, PART_COLS), F32),
         pltpu.VMEM((R, D), F32),
         pltpu.VMEM((R, LANES), F32),
         pltpu.VMEM((n_ep, 2 * req_dev, half + LANES), F32),
         pltpu.VMEM((n_ep, PD, LANES), F32),
-        pltpu.VMEM((n_ep, 2 * PD, half), BF16),
+        pltpu.VMEM((2, n_ep, 2 * PD, PART_COLS), BF16),
         pltpu.VMEM((8, B_COLS), F32),
         pltpu.VMEM((n_ep, 8, B_COLS), F32),
         pltpu.VMEM((n_grp, 2 * slots, half), BF16),
         pltpu.VMEM((CHUNKS, n_grp, 2 * slots, half // CHUNKS), BF16),
-        pltpu.VMEM((CHUNKS, n_grp, 2 * slots, half // CHUNKS), BF16),
+        pltpu.VMEM((CHUNKS, n_grp // 2, 2 * slots, half // CHUNKS), BF16),
+        pltpu.VMEM((CHUNKS, n_grp // 2, 2 * slots, half // CHUNKS), BF16),
+        pltpu.VMEM((CHUNKS, n_grp // 2, 2 * slots, half // CHUNKS), BF16),
         pltpu.VMEM((CHUNKS, n_ep, 2 * cap, half // CHUNKS), F32),
         pltpu.VMEM((CHUNKS, n_ep, 2 * cap, half // CHUNKS), F32),
         dma((2, PD)),
         dma((3,)),
     ]
     for shape in (
-        (n_ep,), (n_ep,), (n_ep,), (n_ep,), (n_grp,), (CHUNKS, n_grp), (CHUNKS, n_ep)
+        (n_ep,), (n_ep,), (2, n_ep), (n_ep,), (n_grp,), (CHUNKS,), (CHUNKS, n_grp // 2),
+        (CHUNKS, n_ep),
     ):
         scratch += [dma(shape), dma(shape)]
     return pl.pallas_call(

time: 40.6 us -> 38.7 us (0.953)
  Pallas kernels: 39.1 us -> 37.1 us
    pallas_call x1, Pallas kernels: 39.1 us -> 37.1 us  [on_device(): pl.pallas_call(functools.partial(fused, (n_grp, n_ep, cap)), out_shape=ja...]
where the time goes in v3:
time: 38.7 us; the launch traced here: 38.4 us
  Pallas kernels  37.1 us (96%)
  local copies, waits for them, and re-layouts  1.34 us (3%)
    pallas_call x1, Pallas kernels, on_device(): pl.pallas_call(functools.partial(fused, (n_grp, n_ep, cap)), out_shape=ja...  37.1 us
    unnamed x1, local copies, waits for them, and re-layouts  1.34 us

profile of v3, /device:TPU:0, one launch (start us, length us, event | category | flops | bytes accessed | tf_op | source)
XLA Modules:
  0.0 38.4 jit_solution(9026909285018176431)
XLA Ops:
  0.0 37.1 %shard_map.127 = bf16[4,2304]{1,0:T(4,128)(2,1)} custom-call(bf16[16,2304]{1,0:T(8,128)(2,1)} %q_ref.1, bf16[4,2304]{1,0:T(4,128)(2,1)} %res_ref.1, bf16[2304]{0:T(1024)(128)(2,1)} %gain_ref.1, s32[16,16]{1,0:T(8,128)} %pt_ref.1, s32[2,4]{1,0:T(2,128)} %bitcast.6, bf16[2,4]{1,0:T(2,128)(2,1)} %bitcast.7, s32[16]{0:T(128)} %len_ref.1, s32[16]{0:T(128)} %split_ref.1, ...), custom_call_target="tpu_custom_call" | custom-call | tf_op jit(solution)/shard_map/pallas_call | solution.py:521
  37.1 1.3 %copy.15 = bf16[4,2304]{1,0:T(4,128)(2,1)} copy(bf16[4,2304]{1,0:T(4,128)(2,1)} %shard_map.127) | data formatting | bytes 36864

commit v4 on v3

--- a/solution.py
+++ b/solution.py
@@ -16,6 +16,7 @@
 TOP = 2
 B_COLS = 384
 CHUNKS = 3
+OCTET = 8
 QUARTERS = ((0, 640), (640, 1280), (1280, 1792), (1792, 2304))
 PART_COLS = 640
 
@@ -38,7 +39,7 @@
     key_hbm, value_hbm, wg_hbm, wu_hbm, wd_hbm,
     out_ref,
     kbuf, vbuf, wg, wu, wd,
-    e_ref, hm_ref, qp_ref, lim_ref, st_ref, w_ref, own_ref, o_ref,
+    e_ref, qp_ref, lim_ref, st_ref, w_ref, own_ref, o_ref,
     wv_ref, af_ref, rs_ref, rt_ref,
     r_all, st_all, a_all, b_send, b_recv, x_all, y_send, y_pair, y_sum, y_recv, z_send, z_recv,
     kv_sem, w_sem,
@@ -51,7 +52,7 @@
     PD = key_hbm.shape[0]
     half = D // 2
     heads = D // HEAD_DIM
-    HP = hm_ref.shape[0]
+    HP = -(-heads // OCTET) * OCTET
     slots = n_ep * cap
     NPP = own_ref.shape[0]
     n_pages = n_ep * PD
@@ -78,15 +79,15 @@
     for peer in [e] + ep_peers:
         pl.semaphore_signal(barrier, inc=1, device_id=(mate, peer), device_id_type=pl.DeviceIdType.MESH)
 
-    def kv_copies(p):
-        return (
-            pltpu.make_async_copy(key_hbm.at[p], kbuf.at[p], kv_sem.at[0, p]),
-            pltpu.make_async_copy(value_hbm.at[p], vbuf.at[p], kv_sem.at[1, p]),
-        )
-
-    for p in range(PD):
-        for copy in kv_copies(p):
-            copy.start()
+    def kv_copy(p, which):
+        source, held = ((key_hbm, kbuf), (value_hbm, vbuf))[which]
+        return pltpu.make_async_copy(source.at[p], held.at[p], kv_sem.at[which, p])
+
+    part_pages = PD // 2
+    for c in range(2):
+        for which in range(2):
+            for p in range(c * part_pages, (c + 1) * part_pages):
+                kv_copy(p, which).start()
     w_copies = [
         pltpu.make_async_copy(wg_hbm.at[0], wg, w_sem.at[0]),
         pltpu.make_async_copy(wu_hbm.at[0], wu, w_sem.at[1]),
@@ -117,20 +118,12 @@
         route_lane[:req_dev] == 0, routes[0],
         jnp.where(route_lane[:req_dev] == 1, routes[1], 0.0),
     )
-    pl.semaphore_wait(barrier, 2 * n_ep - 1 + pairs - 1)
-    r_sends = [
-        remote(r_all.at[e], r_all.at[e], r_ss.at[k], r_rs.at[e], (g, peer))
-        for k, peer in enumerate(ep_peers)
-    ]
-    for copy in r_sends:
-        copy.start()
-
     first_col = iota((LANES, D), 0) * HEAD_DIM
     col = iota((LANES, D), 1)
     in_head = (col >= first_col) & (col < first_col + HEAD_DIM)
     e_ref[...] = jnp.where(in_head, 1.0, 0.0).astype(BF16)
-    hm_ref[...] = jnp.where(in_head[:HP], 1.0, 0.0)
     st_ref[...] = jnp.zeros_like(st_ref)
+    head_mask = jnp.where(in_head[:OCTET, :OCTET * HEAD_DIM], 1.0, 0.0)
     wv_ref[n_pages:, :] = jnp.zeros((NPP - n_pages, D), F32)
 
     split_row = 0
@@ -183,38 +176,59 @@
 
     token = iota((1, LANES), 1).astype(F32)
     stat_lane = iota((HP, LANES), 1)
-
-    def page_step(p):
-        for copy in kv_copies(p):
-            copy.wait()
-        q_page = qp_ref[pl.ds(p, 1), :]
-        q_heads = (jnp.broadcast_to(q_page, (HP, D)) * hm_ref[...]).astype(BF16)
-        scores = dot(q_heads, kbuf[p], ((1,), (1,))) * HEAD_DIM ** (-0.5)
-        visible = token < lim_ref[pl.ds(p, 1), :]
-        scores = jnp.where(visible, scores, NEG_FILL)
+    octets = [
+        (i, i * OCTET * HEAD_DIM, min(D, (i + 1) * OCTET * HEAD_DIM)) for i in range(HP // OCTET)
+    ]
+    af_ref[...] = jnp.zeros_like(af_ref)
+
+    def part(c):
+        first = c * part_pages
+        for p in range(first, first + part_pages):
+            kv_copy(p, 0).wait()
+        scores = []
+        for p in range(first, first + part_pages):
+            rows = []
+            for _, low, high in octets:
+                q_part = jnp.broadcast_to(qp_ref[p:p + 1, low:high], (OCTET, high - low))
+                q_part = (q_part * head_mask[:, :high - low]).astype(BF16)
+                rows.append(dot(q_part, kbuf[p, :, low:high], ((1,), (1,))))
+            visible = token < lim_ref[p:p + 1, :]
+            scores.append(
+                jnp.where(visible, jnp.concatenate(rows, axis=0) * HEAD_DIM ** (-0.5), NEG_FILL)
+            )
+        scores = jnp.concatenate(scores, axis=0)
         top = jnp.maximum(jnp.max(scores, axis=1, keepdims=True), NEG_FLOOR)
         terms = jnp.exp(scores - top)
         total = jnp.sum(terms, axis=1, keepdims=True)
-        st_ref[0:HP, :] = jnp.where(stat_lane == p, top, st_ref[0:HP, :])
-        st_ref[64:64 + HP, :] = jnp.where(stat_lane == p, total, st_ref[64:64 + HP, :])
-        wide = dot(terms.astype(BF16), vbuf[p])
-        w_ref[pl.ds(p, 1), :] = jnp.sum(wide * hm_ref[...], axis=0, keepdims=True)
-
-    def pages(i, carry):
-        page_step(2 * i)
-        page_step(2 * i + 1)
-        return carry
-
-    part_pages = PD // 2
-    af_ref[...] = jnp.zeros_like(af_ref)
-    exchange = []
-
-    def send_part(c):
+        tops, totals = st_ref[0:HP, :], st_ref[64:64 + HP, :]
+        for i in range(part_pages):
+            here = stat_lane == first + i
+            tops = jnp.where(here, top[i * HP:(i + 1) * HP], tops)
+            totals = jnp.where(here, total[i * HP:(i + 1) * HP], totals)
+        st_ref[0:HP, :] = tops
+        st_ref[64:64 + HP, :] = totals
+        for p in range(first, first + part_pages):
+            kv_copy(p, 1).wait()
+        if c:
+            for copy in w_copies:
+                copy.start()
+        for i in range(part_pages):
+            p = first + i
+            for o, low, high in octets:
+                start = i * HP + o * OCTET
+                wide = dot(terms[start:start + OCTET].astype(BF16), vbuf[p, :, low:high])
+                w_ref[p:p + 1, low:high] = jnp.sum(
+                    wide * head_mask[:, :high - low], axis=0, keepdims=True
+                )
         for i, (low, high) in enumerate(QUARTERS):
             af_ref[i * part_pages:(i + 1) * part_pages, 0:high - low] = (
-                w_ref[c * part_pages:(c + 1) * part_pages, low:high]
+                w_ref[first:first + part_pages, low:high]
             )
         a_all[c, e] = af_ref[...].astype(BF16)
+
+    exchange = []
+
+    def send_part(c):
         for k, peer in enumerate(ep_peers):
             copy = remote(
                 a_all.at[c, e], a_all.at[c, e], a_ss.at[c, k], a_rs.at[c, e], (g, peer)
@@ -222,11 +236,16 @@
             copy.start()
             exchange.append(copy)
 
-    lax.fori_loop(0, PD // 4, pages, 0)
+    part(0)
+    pl.semaphore_wait(barrier, 2 * n_ep - 1 + pairs - 1)
+    r_sends = [
+        remote(r_all.at[e], r_all.at[e], r_ss.at[k], r_rs.at[e], (g, peer))
+        for k, peer in enumerate(ep_peers)
+    ]
+    for copy in r_sends:
+        copy.start()
     send_part(0)
-    lax.fori_loop(PD // 4, PD // 2, pages, 0)
-    for copy in w_copies:
-        copy.start()
+    part(1)
     send_part(1)
 
     head_lane = iota((1, LANES), 1) < heads
@@ -242,11 +261,11 @@
     split_top = jnp.max(jnp.where(split_local, stats, NEG_FILL), axis=0, keepdims=True)
     factor = jnp.where(split_local & head_lane, jnp.exp(stats - split_top), 0.0)
     split_total = jnp.sum(factor * totals, axis=0, keepdims=True)
-    part = jnp.sum(dot(factor.astype(BF16), e_ref[...]) * w_ref[...], axis=0, keepdims=True)
+    split_part = jnp.sum(dot(factor.astype(BF16), e_ref[...]) * w_ref[...], axis=0, keepdims=True)
     b_send[...] = jnp.zeros_like(b_send)
     b_rows = D // B_COLS
     for i in range(b_rows):
-        b_send[i:i + 1, :] = part[:, i * B_COLS:(i + 1) * B_COLS]
+        b_send[i:i + 1, :] = split_part[:, i * B_COLS:(i + 1) * B_COLS]
     b_send[b_rows:b_rows + 1, 0:LANES] = split_top
     b_send[b_rows:b_rows + 1, LANES:2 * LANES] = split_total
     b_targets = [e] + ep_peers
@@ -470,8 +489,6 @@
     PD = key_pages.shape[0]
     F = w_gate.shape[2]
     half = D // 2
-    heads = D // HEAD_DIM
-    HP = -(-heads // 8) * 8
     cap = max(2, (TOP * req_dev + n_ep - 1) // n_ep)
     slots = n_ep * cap
     n_pages = n_ep * PD
@@ -487,7 +504,6 @@
         pltpu.VMEM((F, D), BF16),
         pltpu.VMEM((F, D), BF16),
         pltpu.VMEM((LANES, D), BF16),
-        pltpu.VMEM((HP, D), F32),
         pltpu.VMEM((PD, D), F32),
         pltpu.VMEM((PD, LANES), F32),
         pltpu.VMEM((LANES, LANES), F32),

time: 38.7 us -> 37.5 us (0.969)
  Pallas kernels: 37.1 us -> 35.9 us
    pallas_call x1, Pallas kernels: 37.1 us -> 35.9 us  [on_device(): pl.pallas_call(functools.partial(fused, (n_grp, n_ep, cap)), out_shape=ja...]
where the time goes in v4:
time: 37.5 us; the launch traced here: 37.3 us
  Pallas kernels  35.9 us (96%)
  local copies, waits for them, and re-layouts  1.34 us (4%)
    pallas_call x1, Pallas kernels, on_device(): pl.pallas_call(functools.partial(fused, (n_grp, n_ep, cap)), out_shape=ja...  35.9 us
    unnamed x1, local copies, waits for them, and re-layouts  1.34 us

profile of v4, /device:TPU:0, one launch (start us, length us, event | category | flops | bytes accessed | tf_op | source)
XLA Modules:
  0.0 37.3 jit_solution(16559813680239792524)
XLA Ops:
  0.0 35.9 %shard_map.127 = bf16[4,2304]{1,0:T(4,128)(2,1)} custom-call(bf16[16,2304]{1,0:T(8,128)(2,1)} %q_ref.1, bf16[4,2304]{1,0:T(4,128)(2,1)} %res_ref.1, bf16[2304]{0:T(1024)(128)(2,1)} %gain_ref.1, s32[16,16]{1,0:T(8,128)} %pt_ref.1, s32[2,4]{1,0:T(2,128)} %bitcast.6, bf16[2,4]{1,0:T(2,128)(2,1)} %bitcast.7, s32[16]{0:T(128)} %len_ref.1, s32[16]{0:T(128)} %split_ref.1, ...), custom_call_target="tpu_custom_call" | custom-call | tf_op jit(solution)/shard_map/pallas_call | solution.py:537
  35.9 1.3 %copy.15 = bf16[4,2304]{1,0:T(4,128)(2,1)} copy(bf16[4,2304]{1,0:T(4,128)(2,1)} %shard_map.127) | data formatting | bytes 36864

commit v5 on v4

--- a/solution.py
+++ b/solution.py
@@ -17,6 +17,7 @@
 B_COLS = 384
 CHUNKS = 3
 OCTET = 8
+V_COLS = 256
 QUARTERS = ((0, 640), (640, 1280), (1280, 1792), (1792, 2304))
 PART_COLS = 640
 
@@ -123,7 +124,6 @@
     in_head = (col >= first_col) & (col < first_col + HEAD_DIM)
     e_ref[...] = jnp.where(in_head, 1.0, 0.0).astype(BF16)
     st_ref[...] = jnp.zeros_like(st_ref)
-    head_mask = jnp.where(in_head[:OCTET, :OCTET * HEAD_DIM], 1.0, 0.0)
     wv_ref[n_pages:, :] = jnp.zeros((NPP - n_pages, D), F32)
 
     split_row = 0
@@ -174,11 +174,7 @@
         page_q = jnp.where(own_local == float(r), queries[r:r + 1, :], page_q)
     qp_ref[...] = page_q
 
-    token = iota((1, LANES), 1).astype(F32)
-    stat_lane = iota((HP, LANES), 1)
-    octets = [
-        (i, i * OCTET * HEAD_DIM, min(D, (i + 1) * OCTET * HEAD_DIM)) for i in range(HP // OCTET)
-    ]
+    token = iota((PAGE, HP), 0).astype(F32)
     af_ref[...] = jnp.zeros_like(af_ref)
 
     def part(c):
@@ -187,39 +183,29 @@
             kv_copy(p, 0).wait()
         scores = []
         for p in range(first, first + part_pages):
-            rows = []
-            for _, low, high in octets:
-                q_part = jnp.broadcast_to(qp_ref[p:p + 1, low:high], (OCTET, high - low))
-                q_part = (q_part * head_mask[:, :high - low]).astype(BF16)
-                rows.append(dot(q_part, kbuf[p, :, low:high], ((1,), (1,))))
-            visible = token < lim_ref[p:p + 1, :]
-            scores.append(
-                jnp.where(visible, jnp.concatenate(rows, axis=0) * HEAD_DIM ** (-0.5), NEG_FILL)
-            )
-        scores = jnp.concatenate(scores, axis=0)
-        top = jnp.maximum(jnp.max(scores, axis=1, keepdims=True), NEG_FLOOR)
-        terms = jnp.exp(scores - top)
-        total = jnp.sum(terms, axis=1, keepdims=True)
-        tops, totals = st_ref[0:HP, :], st_ref[64:64 + HP, :]
+            q_heads = jnp.broadcast_to(qp_ref[p:p + 1, :].astype(BF16), (HP, D)) * e_ref[0:HP, :]
+            page_scores = dot(kbuf[p], q_heads, ((1,), (1,))) * HEAD_DIM ** (-0.5)
+            scores.append(jnp.where(token < lim_ref[p:p + 1, 0:1], page_scores, NEG_FILL))
+        weights = []
         for i in range(part_pages):
-            here = stat_lane == first + i
-            tops = jnp.where(here, top[i * HP:(i + 1) * HP], tops)
-            totals = jnp.where(here, total[i * HP:(i + 1) * HP], totals)
-        st_ref[0:HP, :] = tops
-        st_ref[64:64 + HP, :] = totals
+            p = first + i
+            top = jnp.maximum(jnp.max(scores[i], axis=0, keepdims=True), NEG_FLOOR)
+            terms = jnp.exp(scores[i] - top)
+            st_ref[p:p + 1, 0:HP] = top
+            st_ref[p:p + 1, 64:64 + HP] = jnp.sum(terms, axis=0, keepdims=True)
+            weights.append(terms.astype(BF16))
+        weights = jnp.concatenate(weights, axis=0)
         for p in range(first, first + part_pages):
             kv_copy(p, 1).wait()
         if c:
             for copy in w_copies:
                 copy.start()
-        for i in range(part_pages):
-            p = first + i
-            for o, low, high in octets:
-                start = i * HP + o * OCTET
-                wide = dot(terms[start:start + OCTET].astype(BF16), vbuf[p, :, low:high])
-                w_ref[p:p + 1, low:high] = jnp.sum(
-                    wide * head_mask[:, :high - low], axis=0, keepdims=True
-                )
+        for low in range(0, D, V_COLS):
+            columns = slice(low, low + V_COLS)
+            spread = dot(weights, e_ref[0:HP, columns]).reshape(part_pages, PAGE, V_COLS)
+            w_ref[first:first + part_pages, columns] = jnp.sum(
+                spread * vbuf[first:first + part_pages, :, columns].astype(F32), axis=1
+            )
         for i, (low, high) in enumerate(QUARTERS):
             af_ref[i * part_pages:(i + 1) * part_pages, 0:high - low] = (
                 w_ref[first:first + part_pages, low:high]
@@ -250,7 +236,7 @@
 
     head_lane = iota((1, LANES), 1) < heads
 
-    stats = jnp.transpose(st_ref[...])[0:PD, :]
+    stats = st_ref[...]
     st_all[e] = stats
     for k, peer in enumerate(ep_peers):
         copy = remote(st_all.at[e], st_all.at[e], st_ss.at[k], st_rs.at[e], (g, peer))
@@ -399,10 +385,11 @@
     rows_in = x_all[...].astype(F32)
     x_lo = rows_in[:, :slots, :].reshape(n_grp * slots, half).astype(BF16)
     x_hi = rows_in[:, slots:, :].reshape(n_grp * slots, half).astype(BF16)
-    last = ((1,), (1,))
-    gate_part = dot(x_lo, wg[:, 0:half], last) + dot(x_hi, wg[:, half:D], last)
-    up_part = dot(x_lo, wu[:, 0:half], last) + dot(x_hi, wu[:, half:D], last)
-    inner = (gate_part / (1.0 + jnp.exp(-gate_part)) * up_part).astype(BF16)
+    x_rows = jnp.concatenate([x_lo, x_hi], axis=1)
+    gate_part = dot(wg[...], x_rows, ((1,), (1,)))
+    up_part = dot(wu[...], x_rows, ((1,), (1,)))
+    inner = gate_part / (1.0 + jnp.exp(-gate_part)) * up_part
+    inner = jnp.transpose(inner).astype(BF16)
 
     width = D // CHUNKS
     piece = width // 2
@@ -506,7 +493,7 @@
         pltpu.VMEM((LANES, D), BF16),
         pltpu.VMEM((PD, D), F32),
         pltpu.VMEM((PD, LANES), F32),
-        pltpu.VMEM((LANES, LANES), F32),
+        pltpu.VMEM((PD, LANES), F32),
         pltpu.VMEM((PD, D), F32),
         pltpu.VMEM((NPP, LANES), F32),
         pltpu.VMEM((R, NPP), BF16),

time: 37.5 us -> 37.7 us (level)
  no operation moved by 1% of the time
where the time goes in v5:
time: 37.7 us; the launch traced here: 37.5 us
  Pallas kernels  36.1 us (96%)
  local copies, waits for them, and re-layouts  1.34 us (4%)
    pallas_call x1, Pallas kernels, on_device(): pl.pallas_call(functools.partial(fused, (n_grp, n_ep, cap)), out_shape=ja...  36.1 us
    unnamed x1, local copies, waits for them, and re-layouts  1.34 us

profile of v5, /device:TPU:0, one launch (start us, length us, event | category | flops | bytes accessed | tf_op | source)
XLA Modules:
  0.0 37.5 jit_solution(13586041138314685543)
XLA Ops:
  0.0 36.1 %shard_map.127 = bf16[4,2304]{1,0:T(4,128)(2,1)} custom-call(bf16[16,2304]{1,0:T(8,128)(2,1)} %q_ref.1, bf16[4,2304]{1,0:T(4,128)(2,1)} %res_ref.1, bf16[2304]{0:T(1024)(128)(2,1)} %gain_ref.1, s32[16,16]{1,0:T(8,128)} %pt_ref.1, s32[2,4]{1,0:T(2,128)} %bitcast.6, bf16[2,4]{1,0:T(2,128)(2,1)} %bitcast.7, s32[16]{0:T(128)} %len_ref.1, s32[16]{0:T(128)} %split_ref.1, ...), custom_call_target="tpu_custom_call" | custom-call | tf_op jit(solution)/shard_map/pallas_call | solution.py:524
  36.1 1.3 %copy.15 = bf16[4,2304]{1,0:T(4,128)(2,1)} copy(bf16[4,2304]{1,0:T(4,128)(2,1)} %shard_map.127) | data formatting | bytes 36864

commit v6 on v5

--- a/solution.py
+++ b/solution.py
@@ -20,6 +20,8 @@
 V_COLS = 256
 QUARTERS = ((0, 640), (640, 1280), (1280, 1792), (1792, 2304))
 PART_COLS = 640
+ROUTE_PART = 2
+ROUTE_COL = 512
 
 F32 = jnp.float32
 BF16 = jnp.bfloat16
@@ -101,10 +103,6 @@
             device_id=device, device_id_type=pl.DeviceIdType.MESH,
         )
 
-    res = res_ref[...].astype(F32)
-    r_all[e, 0:req_dev, 0:half] = res[:, :half]
-    r_all[e, req_dev:2 * req_dev, 0:half] = res[:, half:]
-    route_lane = iota((2 * req_dev, LANES), 1)
     eye = iota((req_dev, req_dev), 0) == iota((req_dev, req_dev), 1)
 
     def column(row):
@@ -114,11 +112,16 @@
     gates_t = gates_ref[...].astype(F32)
     routes = [column(routes_t[k:k + 1, :]) for k in range(TOP)]
     gates = [column(gates_t[k:k + 1, :]) for k in range(TOP)]
-    r_all[e, :, half:half + LANES] = jnp.zeros((2 * req_dev, LANES), F32)
-    r_all[e, 0:req_dev, half:half + LANES] = jnp.where(
-        route_lane[:req_dev] == 0, routes[0],
-        jnp.where(route_lane[:req_dev] == 1, routes[1], 0.0),
+    route_lane = iota((req_dev, LANES), 1)
+    af_ref[...] = jnp.zeros_like(af_ref)
+    res = res_ref[...].astype(F32)
+    for i, (low, high) in enumerate(QUARTERS):
+        af_ref[i * req_dev:(i + 1) * req_dev, 0:high - low] = res[:, low:high]
+    af_ref[ROUTE_PART * req_dev:(ROUTE_PART + 1) * req_dev, ROUTE_COL:PART_COLS] = jnp.where(
+        route_lane == 0, routes[0], jnp.where(route_lane == 1, routes[1], 0.0)
     )
+    r_all[e] = af_ref[...].astype(BF16)
+
     first_col = iota((LANES, D), 0) * HEAD_DIM
     col = iota((LANES, D), 1)
     in_head = (col >= first_col) & (col < first_col + HEAD_DIM)
@@ -175,7 +178,6 @@
     qp_ref[...] = page_q
 
     token = iota((PAGE, HP), 0).astype(F32)
-    af_ref[...] = jnp.zeros_like(af_ref)
 
     def part(c):
         first = c * part_pages
@@ -222,7 +224,6 @@
             copy.start()
             exchange.append(copy)
 
-    part(0)
     pl.semaphore_wait(barrier, 2 * n_ep - 1 + pairs - 1)
     r_sends = [
         remote(r_all.at[e], r_all.at[e], r_ss.at[k], r_rs.at[e], (g, peer))
@@ -230,6 +231,7 @@
     ]
     for copy in r_sends:
         copy.start()
+    part(0)
     send_part(0)
     part(1)
     send_part(1)
@@ -266,9 +268,10 @@
         remote(r_all.at[src], r_all.at[src], r_ss.at[0], r_rs.at[src], (g, src)).wait_recv()
     for s in range(n_ep):
         rows = slice(s * req_dev, (s + 1) * req_dev)
-        rs_ref[rows, 0:half] = r_all[s, 0:req_dev, 0:half]
-        rs_ref[rows, half:D] = r_all[s, req_dev:2 * req_dev, 0:half]
-        rt_ref[rows, :] = r_all[s, 0:req_dev, half:half + LANES]
+        arrived = r_all[s].astype(F32)
+        for i, (low, high) in enumerate(QUARTERS):
+            rs_ref[rows, low:high] = arrived[i * req_dev:(i + 1) * req_dev, 0:high - low]
+        rt_ref[rows, :] = arrived[ROUTE_PART * req_dev:(ROUTE_PART + 1) * req_dev, ROUTE_COL:PART_COLS]
 
     expert = e.astype(F32)
     chosen = rt_ref[...]
@@ -501,7 +504,7 @@
         pltpu.VMEM((2 * PD, PART_COLS), F32),
         pltpu.VMEM((R, D), F32),
         pltpu.VMEM((R, LANES), F32),
-        pltpu.VMEM((n_ep, 2 * req_dev, half + LANES), F32),
+        pltpu.VMEM((n_ep, 4 * req_dev, PART_COLS), BF16),
         pltpu.VMEM((n_ep, PD, LANES), F32),
         pltpu.VMEM((2, n_ep, 2 * PD, PART_COLS), BF16),
         pltpu.VMEM((8, B_COLS), F32),

time: 37.7 us -> 35.4 us (0.939)
  Pallas kernels: 36.1 us -> 33.9 us
    pallas_call x1, Pallas kernels: 36.1 us -> 33.9 us  [on_device(): pl.pallas_call(functools.partial(fused, (n_grp, n_ep, cap)), out_shape=ja...]
where the time goes in v6:
time: 35.4 us; the launch traced here: 35.2 us
  Pallas kernels  33.9 us (96%)
  local copies, waits for them, and re-layouts  1.34 us (4%)
    pallas_call x1, Pallas kernels, on_device(): pl.pallas_call(functools.partial(fused, (n_grp, n_ep, cap)), out_shape=ja...  33.9 us
    unnamed x1, local copies, waits for them, and re-layouts  1.34 us

profile of v6, /device:TPU:0, one launch (start us, length us, event | category | flops | bytes accessed | tf_op | source)
XLA Modules:
  0.0 35.2 jit_solution(12591532215874950411)
XLA Ops:
  0.0 33.9 %shard_map.127 = bf16[4,2304]{1,0:T(4,128)(2,1)} custom-call(bf16[16,2304]{1,0:T(8,128)(2,1)} %q_ref.1, bf16[4,2304]{1,0:T(4,128)(2,1)} %res_ref.1, bf16[2304]{0:T(1024)(128)(2,1)} %gain_ref.1, s32[16,16]{1,0:T(8,128)} %pt_ref.1, s32[2,4]{1,0:T(2,128)} %bitcast.6, bf16[2,4]{1,0:T(2,128)(2,1)} %bitcast.7, s32[16]{0:T(128)} %len_ref.1, s32[16]{0:T(128)} %split_ref.1, ...), custom_call_target="tpu_custom_call" | custom-call | tf_op jit(solution)/shard_map/pallas_call | solution.py:527
  33.9 1.3 %copy.15 = bf16[4,2304]{1,0:T(4,128)(2,1)} copy(bf16[4,2304]{1,0:T(4,128)(2,1)} %shard_map.127) | data formatting | bytes 36864

commit v7 on v6

--- a/solution.py
+++ b/solution.py
@@ -14,7 +14,9 @@
 NEG_FLOOR = -1e29
 NORM_EPS = 1e-06
 TOP = 2
-B_COLS = 384
+B_COLS = 256
+B_ROWS = 16
+STAT_PARTS = 3
 CHUNKS = 3
 OCTET = 8
 V_COLS = 256
@@ -250,12 +252,14 @@
     factor = jnp.where(split_local & head_lane, jnp.exp(stats - split_top), 0.0)
     split_total = jnp.sum(factor * totals, axis=0, keepdims=True)
     split_part = jnp.sum(dot(factor.astype(BF16), e_ref[...]) * w_ref[...], axis=0, keepdims=True)
-    b_send[...] = jnp.zeros_like(b_send)
     b_rows = D // B_COLS
-    for i in range(b_rows):
-        b_send[i:i + 1, :] = split_part[:, i * B_COLS:(i + 1) * B_COLS]
-    b_send[b_rows:b_rows + 1, 0:LANES] = split_top
-    b_send[b_rows:b_rows + 1, LANES:2 * LANES] = split_total
+    rest = jnp.concatenate([split_top, split_total], axis=1)
+    b_parts = [split_part[:, i * B_COLS:(i + 1) * B_COLS] for i in range(b_rows)]
+    for _ in range(STAT_PARTS):
+        b_parts.append(rest.astype(BF16).astype(F32))
+        rest = rest - b_parts[-1]
+    b_parts.append(jnp.zeros((B_ROWS - b_rows - STAT_PARTS, B_COLS), F32))
+    b_send[...] = jnp.concatenate(b_parts, axis=0).astype(BF16)
     b_targets = [e] + ep_peers
     b_sends = [
         remote(b_send, b_recv.at[e], b_ss.at[k], b_rs.at[e], (mate, peer))
@@ -311,13 +315,15 @@
     extra_top = jnp.full((extra, LANES), NEG_FILL, F32)
     extra_total = jnp.zeros((extra, LANES), F32)
     for s in range(n_ep):
-        extra_top = jnp.where(extra_sub == s, b_recv[s, b_rows:b_rows + 1, 0:LANES], extra_top)
-        extra_total = jnp.where(
-            extra_sub == s, b_recv[s, b_rows:b_rows + 1, LANES:2 * LANES], extra_total
-        )
+        arrived = b_recv[s].astype(F32)
+        joined = arrived[b_rows:b_rows + 1, :]
+        for i in range(1, STAT_PARTS):
+            joined = joined + arrived[b_rows + i:b_rows + i + 1, :]
+        extra_top = jnp.where(extra_sub == s, joined[:, 0:LANES], extra_top)
+        extra_total = jnp.where(extra_sub == s, joined[:, LANES:2 * LANES], extra_total)
         for i in range(b_rows):
             row = n_pages + s
-            wv_ref[row:row + 1, i * B_COLS:(i + 1) * B_COLS] = b_recv[s, i:i + 1, :]
+            wv_ref[row:row + 1, i * B_COLS:(i + 1) * B_COLS] = arrived[i:i + 1, :]
     all_stats = st_all[...].reshape(n_pages, LANES)
     all_top = jnp.concatenate([all_stats, extra_top], axis=0)
     all_total = jnp.concatenate([pltpu.roll(all_stats, 64, 1), extra_total], axis=0)
@@ -507,8 +513,8 @@
         pltpu.VMEM((n_ep, 4 * req_dev, PART_COLS), BF16),
         pltpu.VMEM((n_ep, PD, LANES), F32),
         pltpu.VMEM((2, n_ep, 2 * PD, PART_COLS), BF16),
-        pltpu.VMEM((8, B_COLS), F32),
-        pltpu.VMEM((n_ep, 8, B_COLS), F32),
+        pltpu.VMEM((B_ROWS, B_COLS), BF16),
+        pltpu.VMEM((n_ep, B_ROWS, B_COLS), BF16),
         pltpu.VMEM((n_grp, 2 * slots, half), BF16),
         pltpu.VMEM((CHUNKS, n_grp, 2 * slots, half // CHUNKS), BF16),
         pltpu.VMEM((CHUNKS, n_grp // 2, 2 * slots, half // CHUNKS), BF16),

time: 35.4 us -> 35.1 us (level)
  Pallas kernels: 33.9 us -> 33.5 us
where the time goes in v7:
time: 35.1 us; the launch traced here: 34.9 us
  Pallas kernels  33.5 us (95%)
  local copies, waits for them, and re-layouts  1.34 us (4%)
    pallas_call x1, Pallas kernels, on_device(): pl.pallas_call(functools.partial(fused, (n_grp, n_ep, cap)), out_shape=ja...  33.5 us
    unnamed x1, local copies, waits for them, and re-layouts  1.34 us

profile of v7, /device:TPU:0, one launch (start us, length us, event | category | flops | bytes accessed | tf_op | source)
XLA Modules:
  0.0 34.9 jit_solution(2279356292770733895)
XLA Ops:
  0.0 33.5 %shard_map.127 = bf16[4,2304]{1,0:T(4,128)(2,1)} custom-call(bf16[16,2304]{1,0:T(8,128)(2,1)} %q_ref.1, bf16[4,2304]{1,0:T(4,128)(2,1)} %res_ref.1, bf16[2304]{0:T(1024)(128)(2,1)} %gain_ref.1, s32[16,16]{1,0:T(8,128)} %pt_ref.1, s32[2,4]{1,0:T(2,128)} %bitcast.6, bf16[2,4]{1,0:T(2,128)(2,1)} %bitcast.7, s32[16]{0:T(128)} %len_ref.1, s32[16]{0:T(128)} %split_ref.1, ...), custom_call_target="tpu_custom_call" | custom-call | tf_op jit(solution)/shard_map/pallas_call | solution.py:533
  33.6 1.3 %copy.15 = bf16[4,2304]{1,0:T(4,128)(2,1)} copy(bf16[4,2304]{1,0:T(4,128)(2,1)} %shard_map.127) | data formatting | bytes 36864
